TPU v7x, 256 devices: a whole 4x4x8 slice. The times are simulated.
256 devices in a mesh: samp: 16 (over x, y), snp: 16 (over z, core).
Axes of the slice: x: 4, y: 4, z: 8, core: 2. Of those that a mesh axis runs over, the one named last changes fastest.
Arguments:
- genotype: float32 [32768, 8192], P('samp', 'snp'), may hold values from 0 to 2
- effect: float32 [8192, 64], P('snp'), may hold values from -6 to 6
- window_start: int32 [8192], P(('snp', 'samp')), may hold values from 0 to 8191, as said below
- window_end: int32 [8192], P(('snp', 'samp')), may hold values from 1 to 8192, as said below
Outputs:
- band_product: float32 [8192, 64], P(('snp', 'samp'))
Inputs may be any that keep to these rules, and one draw needn't show every extreme that they name: window_start[i] <= i and i - window_start[i] <= 511. i < window_end[i] and window_end[i] - i <= 512; some SNP has a window of exactly 1023 SNPs.
All inputs are finite; a program needn't handle non-finite values.
Results may differ from a plain program's by a relative error of at most 0.0003.
Values sent between devices are 32-bit elements; how exact they have to be, the bound alone decides.
No kernel may reach another device: no remote copies, remote signals or barrier semaphores. Data moves between devices by JAX's collectives and lax.ppermute only.
A program may use at most 64 MiB of HBM per device.

v0:
```python
import jax
import jax.numpy as jnp
from jax import lax
from jax.sharding import PartitionSpec as P

EPSILON = 1e-05


def with_halo(cells, sides, width):
    for axis, dim in sides:
        count = lax.axis_size(axis)
        ends = count - 1
        head = lax.slice_in_dim(cells, 0, width, axis=dim)
        tail = lax.slice_in_dim(cells, cells.shape[dim] - width, cells.shape[dim], axis=dim)
        cells = jnp.concatenate(
            [
                lax.ppermute(tail, axis, [(i, (i + 1) % count) for i in range(ends)]),
                cells,
                lax.ppermute(head, axis, [((i + 1) % count, i) for i in range(ends)]),
            ],
            axis=dim,
        )
    return cells


def body(genotype, effect, window_start, window_end):
    samp_count = lax.axis_size("samp")
    samples_here, block_width = genotype.shape
    row_count = block_width // samp_count
    sample_total = samples_here * samp_count
    row_first = lax.axis_index("samp") * row_count
    block_offset = lax.axis_index("snp") * block_width
    extended = with_halo(genotype, (("snp", 1),), block_width)
    col_index = block_offset - block_width + jnp.arange(3 * block_width, dtype=jnp.int32)
    column_mean = lax.psum(jnp.sum(extended, axis=0), "samp") / sample_total
    centred_sq = jnp.sum((extended - column_mean[None, :]) ** 2, axis=0)
    column_spread = lax.psum(centred_sq, "samp")
    column_scale = lax.rsqrt(column_spread / sample_total + EPSILON)
    whole_sums = lax.psum(
        lax.dot_general(
            genotype,
            extended,
            (((0,), (0,)), ((), ())),
            precision=lax.Precision.HIGHEST,
            preferred_element_type=jnp.float32,
        ),
        "samp",
    )
    cross_products = lax.dynamic_slice_in_dim(whole_sums, row_first, row_count, 0)
    row_mean = lax.dynamic_slice_in_dim(column_mean, block_width + row_first, row_count, 0)
    row_scale = lax.dynamic_slice_in_dim(column_scale, block_width + row_first, row_count, 0)
    correlation = (cross_products / sample_total - row_mean[:, None] * column_mean[None, :]) * (
        row_scale[:, None] * column_scale[None, :]
    )
    in_window = (col_index[None, :] >= window_start[:, None]) & (
        col_index[None, :] < window_end[:, None]
    )
    band_values = jnp.where(in_window, correlation, jnp.float32(0.0))
    wide_effect = with_halo(effect, (("snp", 0),), block_width)
    return jnp.dot(
        band_values,
        wide_effect,
        precision=lax.Precision.HIGHEST,
        preferred_element_type=jnp.float32,
    )


def solution(mesh):
    placed = (P("samp", "snp"), P("snp", None), P(("snp", "samp")), P(("snp", "samp")))
    return jax.shard_map(
        body, mesh=mesh, in_specs=placed, out_specs=P(("snp", "samp"), None), check_vma=False
    )
```

profile of v0, /device:TPU:97, one launch (start us, length us, event | category | flops | bytes accessed | tf_op | source)
XLA Modules:
  0.0 205.6 jit_solution(8368924364113040307)
XLA Ops:
  6.5 5.6 %collective-permute-start = (f32[2048,512]{1,0:T(8,128)}, f32[2048,512]{1,0:T(8,128)S(1)}, u32[]{:S(2)}, u32[]{:S(2)}) collective-permute-start(f32[2048,512]{1,0:T(8,128)} %param.4), channel_id=1, source_target_pairs={{0,1},{1,2},{2,3},{3,4},{4,5},{5,6},{6,7},{7,8},{8,9},{9,10},{10,1... | collective-permute-start | bytes 12582920 | tf_op jit(solution)/shard_map/ppermute | solution.py:17
  12.1 1.9 collective-permute-start.1
  14.0 43.8 %collective-permute-done = f32[2048,512]{1,0:T(8,128)S(1)} collective-permute-done((f32[2048,512]{1,0:T(8,128)}, f32[2048,512]{1,0:T(8,128)S(1)}, u32[]{:S(2)}, u32[]{:S(2)}) %collective-permute-start) | collective-permute-done | bytes 4194336 | tf_op jit(solution)/shard_map/ppermute | solution.py:17
  57.9 0.4 constant_dynamic-update-slice_fusion.2
  58.3 2.6 %constant_dynamic-update-slice_fusion.1 = f32[2048,1536]{1,0:T(8,128)S(1)} fusion(f32[2048,1536]{1,0:T(8,128)S(1)} %constant_dynamic-update-slice_fusion.2, f32[2048,512]{1,0:T(8,128)} %param.4), kind=kLoop, calls=%fused_computation.28 | loop fusion | bytes 8388608
  60.9 2.4 %collective-permute-done.1 = f32[2048,512]{1,0:T(8,128)S(1)} collective-permute-done((f32[2048,512]{1,0:T(8,128)}, f32[2048,512]{1,0:T(8,128)S(1)}, u32[]{:S(2)}, u32[]{:S(2)}) %collective-permute-start.1) | collective-permute-done | bytes 4194336 | tf_op jit(solution)/shard_map/ppermute | solution.py:19
  63.4 0.4 constant_dynamic-update-slice_fusion
  63.8 4.6 %copy-done = f32[2048,1536]{1,0:T(8,128)} copy-done((f32[2048,1536]{1,0:T(8,128)}, f32[2048,1536]{1,0:T(8,128)S(1)}, u32[]{:S(2)}) %copy-start) | copy-done | bytes 12582936
  68.4 22.9 %convolution_bitcast_fusion = f32[512,1536]{1,0:T(8,128)} fusion(f32[2048,1536]{1,0:T(8,128)S(1)} %constant_dynamic-update-slice_fusion, f32[2048,512]{1,0:T(8,128)S(1)} %copy-done.1), kind=kOutput, calls=%fused_computation.1 | convolution fusion | flops 19327352832 | bytes 19922944 | tf_op jit(solution)/shard_map/dot_general | solution.py:40
  91.3 0.0 all-reduce.2.cloned.1.call-update
  91.3 3.1 %collective-permute-start.2 = (f32[512,64]{0,1:T(8,128)S(1)}, f32[512,64]{0,1:T(8,128)S(1)}, u32[]{:S(2)}, u32[]{:S(2)}) collective-permute-start(f32[512,64]{0,1:T(8,128)S(1)} %copy-done.2), channel_id=1, source_target_pairs={{0,1},{1,2},{2,3},{3,4},{4,5},{5,6},{6,7},{7,8},{8,9},{9,10},{10,1... | collective-permute-start | bytes 393224 | tf_op jit(solution)/shard_map/ppermute | solution.py:17
  94.4 1.9 collective-permute-start.3
  96.3 0.0 copy-start.3
  96.3 0.0 copy-start.4
  96.4 5.2 %reduce_sum.18 = f32[1536]{0:T(1024)S(1)} reduce(f32[2048,1536]{1,0:T(8,128)} %copy-done, f32[]{:T(128)} %constant.25.clone.1), dimensions={0}, to_apply=%region_1.0 | reduce | flops 3144192 | bytes 12589060 | tf_op jit(solution)/shard_map/reduce_sum | solution.py:35
  101.6 34.8 %psum.22 = f32[1536]{0:T(1024)S(1)} all-reduce(f32[1536]{0:T(1024)S(1)} %reduce_sum.18), channel_id=1, replica_groups=mesh['samp'=16,'snp'=16] {'samp'}, use_global_device_ids=true, to_apply=%region_2.0 | all-reduce | flops 1536 | bytes 12288 | tf_op jit(solution)/shard_map/psum | solution.py:35
  136.3 0.1 dynamic_slice.10
  136.4 6.0 %multiply_reduce_fusion = f32[1536]{0:T(1024)S(1)} fusion(f32[2048,1536]{1,0:T(8,128)} %copy-done, f32[1536]{0:T(1024)S(1)} %broadcast_multiply_fusion), kind=kLoop, calls=%fused_computation | loop fusion | flops 9435648 | bytes 12595200 | tf_op jit(solution)/shard_map/reduce_sum | solution.py:36
  142.4 29.2 %psum.23 = f32[1536]{0:T(1024)S(1)} all-reduce(f32[1536]{0:T(1024)S(1)} %multiply_reduce_fusion), channel_id=1, replica_groups=mesh['samp'=16,'snp'=16] {'samp'}, use_global_device_ids=true, to_apply=%region_4.0 | all-reduce | flops 1536 | bytes 12288 | tf_op jit(solution)/shard_map/psum | solution.py:37
  171.6 0.1 dynamic_slice.11
  171.7 0.0 collective-permute-done.2
  171.7 0.0 collective-permute-done.3
  171.7 25.1 %all-reduce.2.cloned.1.call-done = f32[512,1536]{1,0:T(8,128)} async-done(((f32[512,1536]{1,0:T(8,128)}), f32[512,1536]{1,0:T(8,128)}) %all-reduce.2.cloned.1.call-update) | async-done | bytes 3145744 | tf_op jit(solution)/shard_map/psum | solution.py:39
  196.8 2.0 fusion
  (11 shorter events, 0.0 us)
Async XLA Ops:
  6.5 190.2 %all-reduce.2.cloned.1.call-start = ((), (), s32[]{:S(2)}) async-start(), calls=%async_computation | async-start | bytes 6291456 | tf_op jit(solution)/shard_map/psum | solution.py:39
  6.5 61.8 %copy-start.1 = (f32[2048,512]{1,0:T(8,128)S(1)}, f32[2048,512]{1,0:T(8,128)}, u32[]{:S(2)}) copy-start(f32[2048,512]{1,0:T(8,128)} %param.4) | copy-start | bytes 12582916
  6.5 51.3 %collective-permute-start = (f32[2048,512]{1,0:T(8,128)}, f32[2048,512]{1,0:T(8,128)S(1)}, u32[]{:S(2)}, u32[]{:S(2)}) collective-permute-start(f32[2048,512]{1,0:T(8,128)} %param.4), channel_id=1, source_target_pairs={{0,1},{1,2},{2,3},{3,4},{4,5},{5,6},{6,7},{7,8},{8,9},{9,10},{10,1... | collective-permute-start | bytes 12582920 | tf_op jit(solution)/shard_map/ppermute | solution.py:17
  12.1 51.2 %collective-permute-start.1 = (f32[2048,512]{1,0:T(8,128)}, f32[2048,512]{1,0:T(8,128)S(1)}, u32[]{:S(2)}, u32[]{:S(2)}) collective-permute-start(f32[2048,512]{1,0:T(8,128)} %param.4), channel_id=1, source_target_pairs={{1,0},{2,1},{3,2},{4,3},{5,4},{6,5},{7,6},{8,7},{9,8},{10,9},{11,1... | collective-permute-start | bytes 12582920 | tf_op jit(solution)/shard_map/ppermute | solution.py:19
  63.8 4.6 %copy-start = (f32[2048,1536]{1,0:T(8,128)}, f32[2048,1536]{1,0:T(8,128)S(1)}, u32[]{:S(2)}) copy-start(f32[2048,1536]{1,0:T(8,128)S(1)} %constant_dynamic-update-slice_fusion) | copy-start | bytes 37748740
  68.4 22.9 %copy-start.2 = (f32[512,64]{0,1:T(8,128)S(1)}, f32[512,64]{0,1:T(8,128)}, u32[]{:S(2)}) copy-start(f32[512,64]{0,1:T(8,128)} %param.5) | copy-start | bytes 393220
  91.3 80.4 %collective-permute-start.2 = (f32[512,64]{0,1:T(8,128)S(1)}, f32[512,64]{0,1:T(8,128)S(1)}, u32[]{:S(2)}, u32[]{:S(2)}) collective-permute-start(f32[512,64]{0,1:T(8,128)S(1)} %copy-done.2), channel_id=1, source_target_pairs={{0,1},{1,2},{2,3},{3,4},{4,5},{5,6},{6,7},{7,8},{8,9},{9,10},{10,1... | collective-permute-start | bytes 393224 | tf_op jit(solution)/shard_map/ppermute | solution.py:17
  94.4 77.3 %collective-permute-start.3 = (f32[512,64]{0,1:T(8,128)S(1)}, f32[512,64]{0,1:T(8,128)S(1)}, u32[]{:S(2)}, u32[]{:S(2)}) collective-permute-start(f32[512,64]{0,1:T(8,128)S(1)} %copy-done.2), channel_id=1, source_target_pairs={{1,0},{2,1},{3,2},{4,3},{5,4},{6,5},{7,6},{8,7},{9,8},{10,9},{11,1... | collective-permute-start | bytes 393224 | tf_op jit(solution)/shard_map/ppermute | solution.py:19
  96.3 100.4 %copy-start.3 = (s32[32]{0:T(128)S(1)}, s32[32]{0:T(128)}, u32[]{:S(2)}) copy-start(s32[32]{0:T(128)} %param.7) | copy-start | bytes 388
  96.3 100.4 %copy-start.4 = (s32[32]{0:T(128)S(1)}, s32[32]{0:T(128)}, u32[]{:S(2)}) copy-start(s32[32]{0:T(128)} %param.6) | copy-start | bytes 388
Sparse Core Ops, SparseCore 0:
  91.4 105.3 all-reduce.1
where the time goes:
time: 208 us; the launch traced here: 206 us
  waiting for transfers between devices  71.3 us (34%)
  blocking collectives  63.9 us (31%)
  matrix products  24.9 us (12%)
  between operations  13.5 us (6%)
  starting transfers between devices  12.5 us (6%)
  other arithmetic  11.2 us (5%)
  local copies, waits for them, and re-layouts  8.26 us (4%)
    ppermute x2, waiting for transfers between devices, with_halo(): lax.ppermute(tail, axis, [(i, (i + 1) % count) for i in range(ends)])  43.8 us
    psum x1, blocking collectives, body(): column_mean = lax.psum(jnp.sum(extended, axis=0), 'samp') / sample_total  34.8 us
    psum x1, blocking collectives, body(): column_spread = lax.psum(centred_sq, 'samp')  29.2 us
    psum x1, waiting for transfers between devices, body(): lax.psum(lax.dot_general(genotype, extended, (((0,), (0,)), ((), ())), pr...  25.1 us
    dot_general x1, matrix products, body(): lax.dot_general(genotype, extended, (((0,), (0,)), ((), ())), precision=l...  22.9 us
    ppermute x2, starting transfers between devices, with_halo(): lax.ppermute(tail, axis, [(i, (i + 1) % count) for i in range(ends)])  8.66 us
    unnamed x12, local copies, waits for them, and re-layouts  7.65 us
    reduce_sum x1, other arithmetic, body(): centred_sq = jnp.sum((extended - column_mean[None, :]) ** 2, axis=0)  5.99 us
  transfers between devices with their start and end apart: 5, of which 3 were waited for; matrix products, arithmetic and copies ran while one was open for 7% of the time, Pallas kernels for 0%

commit v1 on v0

v1 whole, which is shorter than its diff:
```python
import jax
import jax.numpy as jnp
from jax import lax
from jax.sharding import PartitionSpec as P

EPSILON = 1e-05
HIGH = lax.Precision.HIGH
HIGHEST = lax.Precision.HIGHEST


def gram(left, right):
    return lax.dot_general(
        left, right, (((0,), (0,)), ((), ())), precision=HIGH, preferred_element_type=jnp.float32
    )


def full_dot(left, right, left_dim, right_dim):
    return lax.dot_general(
        left,
        right,
        (((left_dim,), (right_dim,)), ((), ())),
        precision=HIGHEST,
        preferred_element_type=jnp.float32,
    )


def body(genotype, effect, window_start, window_end):
    samp_count = lax.axis_size("samp")
    snp_count = lax.axis_size("snp")
    samples_here, width = genotype.shape
    columns = effect.shape[1]
    row_count = width // samp_count
    sample_total = samples_here * samp_count
    half = samples_here // 2
    block = lax.axis_index("snp")
    odd = lax.rem(block, 2)
    chip_pairs = [(i, i ^ 1) for i in range(snp_count)]
    cross_pairs = [(i, i + 1) for i in range(1, snp_count - 1, 2)]
    cross_pairs += [(i + 1, i) for i in range(1, snp_count - 1, 2)]

    sent = lax.dynamic_slice_in_dim(genotype, odd * half, half, 0)
    kept = lax.dynamic_slice_in_dim(genotype, (1 - odd) * half, half, 0)
    across = lax.ppermute(sent, "snp", cross_pairs)
    mate = lax.ppermute(genotype, "snp", chip_pairs)

    shard_mean = jnp.sum(genotype, axis=0) / samples_here
    shard_spread = jnp.sum((genotype - shard_mean[None, :]) ** 2, axis=0)
    pack = jnp.concatenate(
        [
            shard_mean,
            shard_spread,
            window_start.astype(jnp.float32),
            window_end.astype(jnp.float32),
            jnp.zeros((2 * row_count,), jnp.float32),
        ]
    ).reshape(1, -1, 128)
    packs = lax.all_to_all(
        jnp.broadcast_to(pack, (samp_count,) + pack.shape[1:]), "samp", 0, 0
    ).reshape(samp_count, -1)
    means = packs[:, :width]
    spreads = packs[:, width : 2 * width]
    starts = packs[:, 2 * width : 2 * width + row_count].reshape(width)
    ends = packs[:, 2 * width + row_count : 2 * width + 2 * row_count].reshape(width)
    mean = jnp.sum(means, axis=0) / samp_count
    spread = jnp.sum(spreads, axis=0) + samples_here * jnp.sum((means - mean[None, :]) ** 2, axis=0)
    scale = lax.rsqrt(spread / sample_total + EPSILON)
    scaled = effect.T * scale[None, :]
    own_info = jnp.concatenate(
        [scaled, mean[None, :], starts[None, :], ends[None, :], jnp.zeros((5, width), jnp.float32)]
    )
    mate_info = lax.ppermute(own_info, "snp", chip_pairs)
    cross_info = lax.ppermute(own_info, "snp", cross_pairs)

    def column_index(which):
        return (which * width + jnp.arange(width, dtype=jnp.int32)).astype(jnp.float32)

    def masked(products, row_starts, row_ends, column_block):
        index = column_index(column_block)
        inside = (index[None, :] >= row_starts[:, None]) & (index[None, :] < row_ends[:, None])
        return jnp.where(inside, products, jnp.float32(0.0))

    shift = shard_mean - mean
    own_products = gram(genotype - shard_mean[None, :], genotype - shard_mean[None, :])
    own_products = own_products + samples_here * shift[:, None] * shift[None, :]
    mate_products = gram(genotype - mean[None, :], mate - mate_info[columns][None, :])
    cross_products = gram(kept - mean[None, :], across - cross_info[columns][None, :])
    cross_block = block + 2 * odd - 1
    own_sum = (
        full_dot(masked(own_products, starts, ends, block), scaled, 1, 1)
        + full_dot(
            masked(mate_products, starts, ends, block + 1 - 2 * odd), mate_info[:columns], 1, 1
        )
        + full_dot(masked(cross_products, starts, ends, cross_block), cross_info[:columns], 1, 1)
    )
    cross_starts = cross_info[columns + 1]
    cross_ends = cross_info[columns + 2]
    index = column_index(block)
    inside = (index[:, None] >= cross_starts[None, :]) & (index[:, None] < cross_ends[None, :])
    cross_sum = full_dot(jnp.where(inside, cross_products, jnp.float32(0.0)), scaled, 0, 1)
    both = jnp.concatenate([own_sum, cross_sum], axis=1).reshape(samp_count, row_count, 2 * columns)
    parts = jnp.sum(lax.all_to_all(both, "samp", 0, 0), axis=0)
    from_across = lax.ppermute(parts[:, columns:], "snp", cross_pairs)
    row_first = lax.axis_index("samp") * row_count
    row_scale = lax.dynamic_slice_in_dim(scale, row_first, row_count, 0) / sample_total
    return (parts[:, :columns] + from_across) * row_scale[:, None]


def solution(mesh):
    placed = (P("samp", "snp"), P("snp", None), P(("snp", "samp")), P(("snp", "samp")))
    return jax.shard_map(
        body, mesh=mesh, in_specs=placed, out_specs=P(("snp", "samp"), None), check_vma=False
    )
```

time: 208 us -> 85.7 us (0.41)
  blocking collectives: 63.9 us -> 0 us
  waiting for transfers between devices: 71.3 us -> 16.1 us
  starting transfers between devices: 12.5 us -> 30.8 us
  between operations: 13.5 us -> 0.28 us
  other arithmetic: 11.2 us -> 6.15 us
  local copies, waits for them, and re-layouts: 8.26 us -> 3.88 us
  matrix products: 24.9 us -> 28.1 us
    psum x2 -> x0, blocking collectives: 63.9 us -> none  [the longest x1 34.8 us: body(): column_mean = lax.psum(jnp.sum(extended, axis=0), 'samp') / sample_total]
    ppermute x4 -> x5, waiting for transfers between devices: 46.2 us -> 7.61 us  [the longest x1 6.27 us: body(): cross_info = lax.ppermute(own_info, 'snp', cross_pairs)]
    psum x1 -> x0, waiting for transfers between devices: 25.1 us -> none  [body(): lax.psum(lax.dot_general(genotype, extended, (((0,), (0,)), ((), ())), pr...]
    all_to_all x0 -> x2, starting transfers between devices: none -> 13.7 us  [the longest x1 6.92 us: body(): parts = jnp.sum(lax.all_to_all(both, 'samp', 0, 0), axis=0)]
    all_to_all x0 -> x2, waiting for transfers between devices: none -> 8.47 us  [the longest x1 8.47 us: body(): parts = jnp.sum(lax.all_to_all(both, 'samp', 0, 0), axis=0)]
    unnamed x12 -> x9, local copies, waits for them, and re-layouts: 7.65 us -> 0.05 us
    reduce_sum x2 -> x5, other arithmetic: 11.2 us -> 5.32 us  [the longest x1 2.74 us: body(): shard_spread = jnp.sum((genotype - shard_mean[None, :]) ** 2, axis=0)]
    ppermute x4 -> x5, starting transfers between devices: 12.5 us -> 17.1 us  [the longest x1 5.11 us: body(): from_across = lax.ppermute(parts[:, columns:], 'snp', cross_pairs)]
  transfers between devices with their start and end apart: 5 -> 7, of which waited for: 3 -> 3; matrix products, arithmetic and copies ran while one was open for 7% -> 29% of each run, Pallas kernels for 0% -> 0%
where the time goes in v1:
time: 85.7 us; the launch traced here: 85.3 us
  starting transfers between devices  30.8 us (36%)
  matrix products  28.1 us (33%)
  waiting for transfers between devices  16.1 us (19%)
  other arithmetic  6.15 us (7%)
  local copies, waits for them, and re-layouts  3.88 us (5%)
    dot_general x3, matrix products, gram(): lax.dot_general(left, right, (((0,), (0,)), ((), ())), precision=HIGH, pr...  23.5 us
    all_to_all x1, waiting for transfers between devices, body(): parts = jnp.sum(lax.all_to_all(both, 'samp', 0, 0), axis=0)  8.47 us
    all_to_all x1, starting transfers between devices, body(): parts = jnp.sum(lax.all_to_all(both, 'samp', 0, 0), axis=0)  6.92 us
    all_to_all x1, starting transfers between devices, body(): lax.all_to_all(jnp.broadcast_to(pack, (samp_count,) + pack.shape[1:]), 's...  6.75 us
    ppermute x1, waiting for transfers between devices, body(): cross_info = lax.ppermute(own_info, 'snp', cross_pairs)  6.27 us
    ppermute x1, starting transfers between devices, body(): from_across = lax.ppermute(parts[:, columns:], 'snp', cross_pairs)  5.11 us
    ppermute x1, starting transfers between devices, body(): across = lax.ppermute(sent, 'snp', cross_pairs)  4.95 us
    ppermute x1, starting transfers between devices, body(): cross_info = lax.ppermute(own_info, 'snp', cross_pairs)  4.84 us
  transfers between devices with their start and end apart: 7, of which 3 were waited for; matrix products, arithmetic and copies ran while one was open for 29% of the time, Pallas kernels for 0%

profile of v1, /device:TPU:97, one launch (start us, length us, event | category | flops | bytes accessed | tf_op | source)
XLA Modules:
  0.0 85.3 jit_solution(14686827570183099281)
XLA Ops:
  0.0 0.7 collective-permute-start
  0.7 2.5 %reduce_sum.54 = f32[512]{0:T(512)S(1)} reduce(f32[2048,512]{1,0:T(8,128)} %param.4, f32[]{:T(128)} %constant.10.clone.1), dimensions={0}, to_apply=%region_0.0 | reduce | flops 1048064 | bytes 4196356 | tf_op jit(solution)/shard_map/reduce_sum | solution.py:46
  3.3 2.7 %multiply_reduce_fusion = f32[512]{0:T(512)S(1)} fusion(f32[2048,512]{1,0:T(8,128)} %param.4, f32[512]{0:T(512)S(1)} %broadcast_multiply_fusion.2), kind=kLoop, calls=%fused_computation.3 | loop fusion | flops 3145216 | bytes 4198400 | tf_op jit(solution)/shard_map/reduce_sum | solution.py:47
  6.1 0.7 broadcast_in_dim.16
  6.7 6.8 %all-to-all-start = ((f32[16,9,128]{2,1,0:T(8,128)}), f32[16,9,128]{2,1,0:T(8,128)S(1)}, u32[]{:S(2)}, u32[]{:S(2)}) async-start(f32[16,9,128]{2,1,0:T(8,128)} %broadcast_in_dim.16), calls=%async_computation | async-start | bytes 262144 | tf_op jit(solution)/shard_map/all_to_all | solution.py:57
  13.5 1.8 %constant_dynamic-slice_fusion = f32[1024,512]{1,0:T(8,128)S(1)} fusion(f32[2048,512]{1,0:T(8,128)} %param.4, s32[]{:T(128)S(6)} %select_n.25), kind=kLoop, calls=%fused_computation.60 | loop fusion | bytes 4194308 | tf_op jit(solution)/shard_map/dynamic_slice | solution.py:41
  15.3 4.9 %collective-permute-start.2 = (f32[1024,512]{1,0:T(8,128)S(1)}, f32[1024,512]{1,0:T(8,128)}, u32[]{:S(2)}, u32[]{:S(2)}) collective-permute-start(f32[1024,512]{1,0:T(8,128)S(1)} %constant_dynamic-slice_fusion), channel_id=1, source_target_pairs={{1,2},{3,4},{5,6},{7,8},{9,10},{11,12},{13,14},{2,1},{4,3},{6,5},{... | collective-permute-start | bytes 6291464 | tf_op jit(solution)/shard_map/ppermute | solution.py:43
  20.9 1.5 %collective-permute-start.1 = (f32[72,512]{1,0:T(8,128)S(1)}, f32[72,512]{1,0:T(8,128)S(1)}, u32[]{:S(2)}, u32[]{:S(2)}) collective-permute-start(f32[72,512]{1,0:T(8,128)S(1)} %concatenate.10), channel_id=1, source_target_pairs={{0,1},{1,0},{2,3},{3,2},{4,5},{5,4},{6,7},{7,6},{8,9},{9,8},{10,11... | collective-permute-start | bytes 442376 | tf_op jit(solution)/shard_map/ppermute | solution.py:71
  22.4 4.8 %collective-permute-start.3 = (f32[72,512]{1,0:T(8,128)S(1)}, f32[72,512]{1,0:T(8,128)S(1)}, u32[]{:S(2)}, u32[]{:S(2)}) collective-permute-start(f32[72,512]{1,0:T(8,128)S(1)} %concatenate.10), channel_id=1, source_target_pairs={{1,2},{3,4},{5,6},{7,8},{9,10},{11,12},{13,14},{2,1},{4,3},{6,5},{... | collective-permute-start | bytes 442376 | tf_op jit(solution)/shard_map/ppermute | solution.py:72
  27.3 10.8 %fusion.15 = f32[512,512]{1,0:T(8,128)S(1)} fusion(f32[2048,512]{1,0:T(8,128)} %param.4, f32[512]{0:T(512)S(1)} %broadcast_multiply_fusion.2, f32[512]{0:T(512)S(1)} %get-tuple-element.8, f32[512]{0:T(512)S(1)} %get-tuple-element.7, f32[512]{0:T(512)S(1)} %add_convert_fusion.2, f32[512]{0:T(512)S(1)} %lt.22, f32[512]{0:T(512)S(1)} %ge.25), kind=kOutput, calls=%fused_computation.14 | convolution fusion | flops 3223846912 | bytes 5255168 | tf_op jit(solution)/shard_map/dot_general | solution.py:12
  38.1 1.1 %fusion.45 = f32[512,64]{0,1:T(8,128)S(1)} fusion(f32[512,512]{1,0:T(8,128)S(1)} %fusion.15, f32[512,64]{0,1:T(8,128)S(1)} %copy-done.1, f32[512]{0:T(512)S(1)} %add_rsqrt_fusion), kind=kOutput, calls=%fused_computation.42 | convolution fusion | flops 201359360 | bytes 1312768 | tf_op jit(solution)/shard_map/dot_general | solution.py:18
  39.2 6.3 %collective-permute-done.3 = f32[72,512]{1,0:T(8,128)S(1)} collective-permute-done((f32[72,512]{1,0:T(8,128)S(1)}, f32[72,512]{1,0:T(8,128)S(1)}, u32[]{:S(2)}, u32[]{:S(2)}) %collective-permute-start.3) | collective-permute-done | bytes 147488 | tf_op jit(solution)/shard_map/ppermute | solution.py:72
  45.5 3.5 %fusion.5 = f32[512,512]{1,0:T(8,128)S(1)} fusion(f32[1024,512]{1,0:T(8,128)} %collective-permute-done.2, f32[2048,512]{1,0:T(8,128)S(1)} %copy-done, s32[]{:T(128)S(6)} %select_n.24, f32[512]{0:T(512)S(1)} %bitcast.24, f32[512]{0:T(512)S(1)} %get-tuple-element.14), kind=kOutput, calls=%fused_computation.6 | convolution fusion | flops 1611661312 | bytes 5246980 | tf_op jit(solution)/shard_map/dot_general | solution.py:12
  49.0 1.0 %fusion.23 = f32[512,64]{0,1:T(8,128)S(1)} fusion(f32[512,512]{1,0:T(8,128)S(1)} %fusion.5, f32[512]{0:T(512)S(1)} %bitcast.23, f32[512]{0:T(512)S(1)} %bitcast.22, f32[512]{0:T(512)S(1)} %add_convert_fusion.2, f32[512,64]{0,1:T(8,128)S(1)} %copy-done.1, f32[512]{0:T(512)S(1)} %add_rsqrt_fusion), kind=kOutput, calls=%fused_computation.18 | convolution fusion | flops 202407936 | bytes 1318912 | tf_op jit(solution)/shard_map/dot_general | solution.py:18
  50.0 9.2 %fusion.18 = f32[512,512]{1,0:T(8,128)S(1)} fusion(f32[2048,512]{1,0:T(8,128)} %collective-permute-done, f32[512]{0:T(512)S(1)} %bitcast.21, f32[2048,512]{1,0:T(8,128)S(1)} %copy-done, f32[512]{0:T(512)S(1)} %get-tuple-element.14, f32[512]{0:T(512)S(1)} %add_convert_fusion.1, f32[512]{0:T(512)S(1)} %lt.22, f32[512]{0:T(512)S(1)} %ge.25), kind=kOutput, calls=%fused_computation.15 | convolution fusion | flops 3224371200 | bytes 9447424 | tf_op jit(solution)/shard_map/dot_general | solution.py:12
  59.3 1.1 %convolution_add_fusion.1 = f32[512,64]{0,1:T(8,128)S(1)} fusion(f32[512,64]{0,1:T(8,128)S(1)} %fusion.45, f32[512,512]{1,0:T(8,128)S(1)} %fusion.18, f32[72,512]{1,0:T(8,128)S(1)} %collective-permute-done.1), kind=kOutput, calls=%fused_computation.17 | convolution fusion | flops 201359360 | bytes 1441792 | tf_op jit(solution)/shard_map/dot_general | solution.py:18
  60.4 1.3 %convolution_add_fusion = f32[512,64]{0,1:T(8,128)S(1)} fusion(f32[512,64]{0,1:T(8,128)S(1)} %convolution_add_fusion.1, f32[512,512]{1,0:T(8,128)S(1)} %fusion.5, f32[512]{0:T(512)S(1)} %add_convert_fusion, f32[512]{0:T(512)S(1)} %lt.22, f32[512]{0:T(512)S(1)} %ge.25, f32[72,512]{1,0:T(8,128)S(1)} %collective-permute-done.3), kind=kOutput, calls=%fused_computation.16 | convolution fusion | flops 202407936 | bytes 1447936 | tf_op jit(solution)/shard_map/dot_general | solution.py:18
  61.8 0.8 copy.5
  62.6 6.9 %all-to-all-start.1 = ((f32[16,32,128]{2,1,0:T(8,128)}), f32[16,32,128]{2,1,0:T(8,128)S(1)}, u32[]{:S(2)}, u32[]{:S(2)}) async-start(f32[16,32,128]{2,1,0:T(8,128)} %bitcast.7), calls=%async_computation.1 | async-start | bytes 524288 | tf_op jit(solution)/shard_map/all_to_all | solution.py:101
  69.5 8.5 %all-to-all-done.1 = f32[16,32,128]{2,1,0:T(8,128)S(1)} async-done(((f32[16,32,128]{2,1,0:T(8,128)}), f32[16,32,128]{2,1,0:T(8,128)S(1)}, u32[]{:S(2)}, u32[]{:S(2)}) %all-to-all-start.1) | async-done | bytes 262176 | tf_op jit(solution)/shard_map/all_to_all | solution.py:101
  78.1 5.1 %collective-permute-start.4 = (f32[32,64]{1,0:T(8,128)S(1)}, f32[32,64]{1,0:T(8,128)S(1)}, u32[]{:S(2)}, u32[]{:S(2)}) collective-permute-start(f32[32,64]{1,0:T(8,128)S(1)} %slice.59), channel_id=1, source_target_pairs={{1,2},{3,4},{5,6},{7,8},{9,10},{11,12},{13,14},{2,1},{4,3},{6,5},{... | collective-permute-start | bytes 24584 | tf_op jit(solution)/shard_map/ppermute | solution.py:102
  83.2 0.1 dynamic-slice_multiply_fusion
  83.3 1.3 %collective-permute-done.4 = f32[32,64]{1,0:T(8,128)S(1)} collective-permute-done((f32[32,64]{1,0:T(8,128)S(1)}, f32[32,64]{1,0:T(8,128)S(1)}, u32[]{:S(2)}, u32[]{:S(2)}) %collective-permute-start.4) | collective-permute-done | bytes 8224 | tf_op jit(solution)/shard_map/ppermute | solution.py:102
  84.6 0.7 fusion.49
  (38 shorter events, 0.8 us)
Async XLA Ops:
  0.0 3.2 %copy-start.2 = (s32[32]{0:T(128)S(1)}, s32[32]{0:T(128)}, u32[]{:S(2)}) copy-start(s32[32]{0:T(128)} %param.6) | copy-start | bytes 388
  0.0 3.2 %copy-start.3 = (s32[32]{0:T(128)S(1)}, s32[32]{0:T(128)}, u32[]{:S(2)}) copy-start(s32[32]{0:T(128)} %param.7) | copy-start | bytes 388
  0.0 50.0 %collective-permute-start = (f32[2048,512]{1,0:T(8,128)}, f32[2048,512]{1,0:T(8,128)}, u32[]{:S(2)}, u32[]{:S(2)}) collective-permute-start(f32[2048,512]{1,0:T(8,128)} %param.4), channel_id=1, source_target_pairs={{0,1},{1,0},{2,3},{3,2},{4,5},{5,4},{6,7},{7,6},{8,9},{9,8},{10,11... | collective-permute-start | bytes 12582920 | tf_op jit(solution)/shard_map/ppermute | solution.py:44
  3.2 17.6 %copy-start.1 = (f32[512,64]{0,1:T(8,128)S(1)}, f32[512,64]{0,1:T(8,128)}, u32[]{:S(2)}) copy-start(f32[512,64]{0,1:T(8,128)} %param.5) | copy-start | bytes 393220
  6.7 13.6 %all-to-all-start = ((f32[16,9,128]{2,1,0:T(8,128)}), f32[16,9,128]{2,1,0:T(8,128)S(1)}, u32[]{:S(2)}, u32[]{:S(2)}) async-start(f32[16,9,128]{2,1,0:T(8,128)} %broadcast_in_dim.16), calls=%async_computation | async-start | bytes 262144 | tf_op jit(solution)/shard_map/all_to_all | solution.py:57
  15.3 30.2 %collective-permute-start.2 = (f32[1024,512]{1,0:T(8,128)S(1)}, f32[1024,512]{1,0:T(8,128)}, u32[]{:S(2)}, u32[]{:S(2)}) collective-permute-start(f32[1024,512]{1,0:T(8,128)S(1)} %constant_dynamic-slice_fusion), channel_id=1, source_target_pairs={{1,2},{3,4},{5,6},{7,8},{9,10},{11,12},{13,14},{2,1},{4,3},{6,5},{... | collective-permute-start | bytes 6291464 | tf_op jit(solution)/shard_map/ppermute | solution.py:43
  20.9 18.4 %collective-permute-start.1 = (f32[72,512]{1,0:T(8,128)S(1)}, f32[72,512]{1,0:T(8,128)S(1)}, u32[]{:S(2)}, u32[]{:S(2)}) collective-permute-start(f32[72,512]{1,0:T(8,128)S(1)} %concatenate.10), channel_id=1, source_target_pairs={{0,1},{1,0},{2,3},{3,2},{4,5},{5,4},{6,7},{7,6},{8,9},{9,8},{10,11... | collective-permute-start | bytes 442376 | tf_op jit(solution)/shard_map/ppermute | solution.py:71
  22.4 23.1 %collective-permute-start.3 = (f32[72,512]{1,0:T(8,128)S(1)}, f32[72,512]{1,0:T(8,128)S(1)}, u32[]{:S(2)}, u32[]{:S(2)}) collective-permute-start(f32[72,512]{1,0:T(8,128)S(1)} %concatenate.10), channel_id=1, source_target_pairs={{1,2},{3,4},{5,6},{7,8},{9,10},{11,12},{13,14},{2,1},{4,3},{6,5},{... | collective-permute-start | bytes 442376 | tf_op jit(solution)/shard_map/ppermute | solution.py:72
  27.3 18.3 %copy-start = (f32[2048,512]{1,0:T(8,128)S(1)}, f32[2048,512]{1,0:T(8,128)}, u32[]{:S(2)}) copy-start(f32[2048,512]{1,0:T(8,128)} %param.4) | copy-start | bytes 12582916
  62.6 15.4 %all-to-all-start.1 = ((f32[16,32,128]{2,1,0:T(8,128)}), f32[16,32,128]{2,1,0:T(8,128)S(1)}, u32[]{:S(2)}, u32[]{:S(2)}) async-start(f32[16,32,128]{2,1,0:T(8,128)} %bitcast.7), calls=%async_computation.1 | async-start | bytes 524288 | tf_op jit(solution)/shard_map/all_to_all | solution.py:101
  78.1 6.5 %collective-permute-start.4 = (f32[32,64]{1,0:T(8,128)S(1)}, f32[32,64]{1,0:T(8,128)S(1)}, u32[]{:S(2)}, u32[]{:S(2)}) collective-permute-start(f32[32,64]{1,0:T(8,128)S(1)} %slice.59), channel_id=1, source_target_pairs={{1,2},{3,4},{5,6},{7,8},{9,10},{11,12},{13,14},{2,1},{4,3},{6,5},{... | collective-permute-start | bytes 24584 | tf_op jit(solution)/shard_map/ppermute | solution.py:102

commit v2 on v0

v2 whole, which is shorter than its diff:
```python
import functools

import jax
import jax.numpy as jnp
from jax import lax
from jax.experimental import pallas as pl
from jax.experimental.pallas import tpu as pltpu
from jax.sharding import PartitionSpec as P

EPSILON = 1e-05
F32 = jnp.float32
LANES = 128
LAST_ROWS = 256
STEP_ROWS = 1024
VMEM = pl.BlockSpec(memory_space=pltpu.VMEM)
SMEM = pl.BlockSpec(memory_space=pltpu.SMEM)
ANY = pl.BlockSpec(memory_space=pl.ANY)


def split(values):
    high = values.astype(jnp.bfloat16)
    return high, (values - high.astype(F32)).astype(jnp.bfloat16)


def dot(left, right, left_dim, right_dim):
    return lax.dot_general(
        left, right, (((left_dim,), (right_dim,)), ((), ())), preferred_element_type=F32
    )


def three_dots(left, right, left_dim, right_dim):
    (left_high, left_low), (right_high, right_low) = left, right
    return (
        dot(left_high, right_high, left_dim, right_dim)
        + dot(left_high, right_low, left_dim, right_dim)
        + dot(left_low, right_high, left_dim, right_dim)
    )


def column_means(ref, start, rows):
    return jnp.sum(ref[pl.ds(start, rows), :], axis=0, keepdims=True) / rows


def stat_kernel(place, geno, starts, ends, sent, pack, means):
    del sent
    rows, width = geno.shape
    values = geno[...]
    mean = jnp.sum(values, axis=0, keepdims=True) / rows
    spread = jnp.sum((values - mean) ** 2, axis=0, keepdims=True)
    means[...] = jnp.broadcast_to(mean, means.shape)
    tiles = width // LANES
    here = starts.shape[1]
    slot = (
        lax.broadcasted_iota(jnp.int32, (tiles, LANES), 0) * (LANES // here)
        + lax.broadcasted_iota(jnp.int32, (tiles, LANES), 1) // here
    )
    mine = slot == place[0]

    def spread_out(ref):
        row = jnp.concatenate([ref[...].astype(F32)] * (LANES // here), axis=1)
        return jnp.where(mine, jnp.broadcast_to(row, (tiles, LANES)), jnp.float32(0.0))

    rows_out = [vector[:, t * LANES : (t + 1) * LANES] for vector in (mean, spread) for t in range(tiles)]
    rows_out += [spread_out(starts), spread_out(ends)]
    pack[...] = jnp.broadcast_to(jnp.concatenate(rows_out, axis=0)[None], pack.shape)


def combine_kernel(place, packs, geno, effect, own_products, later, own, *, samples_here):
    del own_products
    count, _, _ = packs.shape
    width = geno.shape[1]
    columns = effect.shape[0]
    tiles = width // LANES
    total = samples_here * count
    values = packs[...]
    means = values[:, :tiles]
    mean = jnp.sum(means, axis=0) / count
    spread = jnp.sum(values[:, tiles : 2 * tiles], axis=0)
    spread = spread + samples_here * jnp.sum((means - mean[None]) ** 2, axis=0)
    scale = lax.rsqrt(spread / total + EPSILON)
    starts = jnp.sum(values[:, 2 * tiles : 3 * tiles], axis=0)
    ends = jnp.sum(values[:, 3 * tiles :], axis=0)

    def as_row(tiled):
        return jnp.concatenate([tiled[t : t + 1] for t in range(tiles)], axis=1)

    info = jnp.concatenate(
        [as_row(mean), as_row(scale), as_row(starts), as_row(ends), jnp.zeros((4, width), F32)], axis=0
    )
    own[:columns] = effect[...]
    own[columns:] = info
    rows = later.shape[0] - own.shape[0]
    begin = pl.multiple_of(place[3], 8)
    later[:rows] = geno[pl.ds(begin, rows), :]
    later[rows : rows + columns] = effect[...]
    later[rows + columns :] = info


def own_kernel(geno, means, products, cross):
    rows = geno.shape[0]
    mean = means[:1]
    products[...] = jnp.zeros_like(products)
    cross[...] = jnp.zeros_like(cross)

    def step(i, carry):
        high, low = split(geno[pl.ds(pl.multiple_of(i * STEP_ROWS, STEP_ROWS), STEP_ROWS), :] - mean)
        products[...] += dot(high, high, 0, 0)
        cross[...] += dot(high, low, 0, 0)
        return carry

    lax.fori_loop(0, rows // STEP_ROWS, step, 0)
    products[...] += cross[...] + cross[...].T


def accumulate(products, left, right, reaches_right):
    half = products.shape[0] // 2
    low, high = slice(0, half), slice(half, 2 * half)
    every = slice(0, 2 * half)

    def add(rows, cols):
        part = three_dots(
            [piece[:, rows] for piece in left], [piece[:, cols] for piece in right], 0, 0
        )
        products[rows, cols] += part

    @pl.when(reaches_right)
    def _():
        add(every, low)
        add(high, high)

    @pl.when(jnp.logical_not(reaches_right))
    def _():
        add(low, every)
        add(high, high)


def pair_kernel(place, geno, other, products, means, *, start_at, right_parity):
    rows = other.shape[0]
    step_rows = min(rows, STEP_ROWS)
    begin = 0 if start_at is None else pl.multiple_of(place[start_at], 8)
    own_mean = column_means(geno, begin, rows)
    other_mean = column_means(other, 0, rows)
    means[...] = jnp.concatenate(
        [own_mean, other_mean, jnp.zeros((6, means.shape[1]), F32)], axis=0
    )
    products[...] = jnp.zeros_like(products)

    def step(i, carry):
        offset = pl.multiple_of(i * step_rows, step_rows)
        left = split(geno[pl.ds(begin + offset, step_rows), :] - own_mean)
        right = split(other[pl.ds(offset, step_rows), :] - other_mean)
        accumulate(products, left, right, place[1] == right_parity)
        return carry

    lax.fori_loop(0, rows // step_rows, step, 0)


def inside(first, shape, dim, starts, ends):
    index = (first + lax.broadcasted_iota(jnp.int32, shape, dim)).astype(F32)
    return (index >= starts) & (index < ends)


def near_kernel(
    place, own_products, means, mate_products, mate_means, own, mate, out, *, columns, samples_here, total
):
    width = own_products.shape[0]
    block, odd = place[2], place[1]
    info = own[columns : columns + 4]
    mean, scale = info[0:1], info[1:2]
    mate_mean, mate_scale = mate[columns : columns + 1], mate[columns + 1 : columns + 2]
    shift = means[0:1] - mean
    mate_side = mate_means[0:1] - mean
    across = jnp.concatenate([info, shift, mate_side, jnp.zeros((2, width), F32)], axis=0).T
    row_scale = across[:, 1:2] * (1.0 / total)
    starts, ends = across[:, 2:3], across[:, 3:4]

    def part(products, row_shift, col_shift, col_scale, block_at, source):
        centred = products[...] + (samples_here * row_shift) * col_shift
        keep = inside(block_at * width, (width, width), 1, starts, ends)
        band = jnp.where(keep, centred * (row_scale * col_scale), jnp.float32(0.0))
        return three_dots(split(band), split(source[:columns]), 1, 1)

    out[...] = part(own_products, across[:, 4:5], shift, scale, block, own) + part(
        mate_products,
        across[:, 5:6],
        mate_means[1:2] - mate_mean,
        mate_scale,
        block + 1 - 2 * odd,
        mate,
    )


def far_kernel(
    place, geno, products_in, means, later, own, near, out, products, *, columns, first_rows, total
):
    width = own.shape[1]
    block, odd = place[2], place[1]
    rows = later.shape[0] - own.shape[0]
    begin = pl.multiple_of(place[5], 8)
    mean = own[columns : columns + 1]
    info = later[rows + columns : rows + columns + 4]
    far_mean, far_scale = info[0:1], info[1:2]
    products[...] = products_in[...]
    left = split(geno[pl.ds(begin, rows), :] - mean)
    right = split(later[:rows] - far_mean)
    accumulate(products, left, right, odd == 1)
    row_shift = means[0:1] - mean
    col_shift = means[1:2] - far_mean
    across = jnp.concatenate(
        [own[columns : columns + 4], row_shift, jnp.zeros((3, width), F32)], axis=0
    ).T
    centred = products[...] + (first_rows * across[:, 4:5]) * col_shift
    correlation = centred * ((across[:, 1:2] * (1.0 / total)) * far_scale)
    shape = (width, width)
    far_block = block + 2 * odd - 1
    keep_own = inside(far_block * width, shape, 1, across[:, 2:3], across[:, 3:4])
    keep_far = inside(block * width, shape, 0, info[2:3], info[3:4])
    own_band = jnp.where(keep_own, correlation, jnp.float32(0.0))
    far_band = jnp.where(keep_far, correlation, jnp.float32(0.0))
    own_sum = near[...] + three_dots(
        split(own_band), split(later[rows : rows + columns]), 1, 1
    )
    far_sum = three_dots(split(own[:columns]), split(far_band), 1, 0).T
    count, _, piece_rows, lanes = out.shape

    def pieces(values):
        parts = values.reshape(count, 2, piece_rows, columns)
        return jnp.concatenate([parts[:, 0], parts[:, 1]], axis=-1)

    out[:, 1 - odd] = pieces(own_sum)
    out[:, odd] = pieces(far_sum)


def last_kernel(parts, out):
    total = jnp.sum(parts[...], axis=0)
    rows, columns = out.shape
    out[: rows // 2] = total[:, :columns]
    out[rows // 2 :] = total[:, columns:]


def call(kernel, shapes, specs, scratch=(), flops=1000, **sizes):
    outs = [jax.ShapeDtypeStruct(shape, F32) for shape in shapes]
    return pl.pallas_call(
        functools.partial(kernel, **sizes),
        out_shape=outs,
        in_specs=specs,
        out_specs=[VMEM] * len(outs),
        scratch_shapes=list(scratch),
        compiler_params=pltpu.CompilerParams(vmem_limit_bytes=40 * 1024 * 1024),
        cost_estimate=pl.CostEstimate(flops=flops, bytes_accessed=1000, transcendentals=0),
        name=kernel.__name__,
    )


def body(genotype, effect, window_start, window_end):
    samp_count = lax.axis_size("samp")
    snp_count = lax.axis_size("snp")
    samples_here, width = genotype.shape
    columns = effect.shape[1]
    row_count = width // samp_count
    total = samples_here * samp_count
    half = samples_here // 2
    first_rows = half - LAST_ROWS
    info_rows = columns + 8
    gram_flops = 6 * width * width * samples_here
    samp = lax.axis_index("samp")
    block = lax.axis_index("snp")
    odd = lax.rem(block, 2)
    sent_at = odd * half
    kept_at = (1 - odd) * half
    place = jnp.stack(
        [samp, odd, block, sent_at + first_rows, kept_at, kept_at + first_rows]
    ).astype(jnp.int32)
    chip_pairs = [(i, i ^ 1) for i in range(snp_count)]
    cross = [(i, (i + 1) % snp_count) for i in range(1, snp_count, 2)]
    cross_pairs = [pair for i, j in cross[:-1] for pair in ((i, j), (j, i))]
    effect_rows = effect.T

    sent = lax.dynamic_slice_in_dim(genotype, sent_at, first_rows, 0)
    first = lax.ppermute(sent, "snp", cross_pairs)
    mate = lax.ppermute(genotype, "snp", chip_pairs)
    pack, means = call(
        stat_kernel,
        [(samp_count, 4 * width // LANES, LANES), (8, width)],
        [SMEM, VMEM, VMEM, VMEM, ANY],
    )(place, genotype, window_start[None], window_end[None], sent)
    packs = lax.all_to_all(pack, "samp", 0, 0)
    own_products = call(
        own_kernel, [(width, width)], [VMEM] * 2, [pltpu.VMEM((width, width), F32)], flops=gram_flops
    )(genotype, means)[0]
    mate_products, mate_means = call(
        pair_kernel,
        [(width, width), (8, width)],
        [SMEM] + [VMEM] * 2,
        start_at=None,
        right_parity=0,
        flops=gram_flops,
    )(place, genotype, mate)
    later, own = call(
        combine_kernel,
        [(LAST_ROWS + info_rows, width), (info_rows, width)],
        [SMEM] + [VMEM] * 3 + [ANY],
        samples_here=samples_here,
    )(place, packs, genotype, effect_rows, own_products)
    later = lax.ppermute(later, "snp", cross_pairs)
    mate_info = lax.ppermute(own, "snp", chip_pairs)
    near = call(
        near_kernel,
        [(width, columns)],
        [SMEM] + [VMEM] * 6,
        columns=columns,
        samples_here=samples_here,
        total=total,
    )(place, own_products, means, mate_products, mate_means, own, mate_info)[0]
    first_products, first_means = call(
        pair_kernel,
        [(width, width), (8, width)],
        [SMEM] + [VMEM] * 2,
        start_at=4,
        right_parity=1,
    )(place, genotype, first)
    sums = call(
        far_kernel,
        [(samp_count, 2, row_count // 2, 2 * columns)],
        [SMEM] + [VMEM] * 6,
        [pltpu.VMEM((width, width), F32)],
        columns=columns,
        first_rows=first_rows,
        total=total,
    )(place, genotype, first_products, first_means, later, own, near)[0]
    groups = [[s * snp_count + i for s in range(samp_count) for i in pair] for pair in cross]
    parts = lax.all_to_all(
        sums.reshape(2 * samp_count, row_count // 2, 2 * columns),
        ("samp", "snp"),
        0,
        0,
        axis_index_groups=groups,
    )
    return call(last_kernel, [(row_count, columns)], [VMEM])(parts)[0]


def solution(mesh):
    placed = (P("samp", "snp"), P("snp", None), P(("snp", "samp")), P(("snp", "samp")))
    return jax.shard_map(
        body, mesh=mesh, in_specs=placed, out_specs=P(("snp", "samp"), None), check_vma=False
    )
```

time: 208 us -> 67.5 us (0.32)
  waiting for transfers between devices: 71.3 us -> 1.43 us
  blocking collectives: 63.9 us -> 16 us
  matrix products: 24.9 us -> 0 us
  Pallas kernels: 0 us -> 23.5 us
  between operations: 13.5 us -> 0.15 us
  other arithmetic: 11.2 us -> 0 us
  starting transfers between devices: 12.5 us -> 16.4 us
    psum x2 -> x0, blocking collectives: 63.9 us -> none  [the longest x1 34.8 us: body(): column_mean = lax.psum(jnp.sum(extended, axis=0), 'samp') / sample_total]
    ppermute x4, waiting for transfers between devices: 46.2 us -> 0.01 us  [the longest x1 0.01 us: body(): mate = lax.ppermute(genotype, 'snp', chip_pairs)]
    psum x1 -> x0, waiting for transfers between devices: 25.1 us -> none  [body(): lax.psum(lax.dot_general(genotype, extended, (((0,), (0,)), ((), ())), pr...]
    dot_general x2 -> x0, matrix products: 24.9 us -> none  [the longest x1 22.9 us: body(): lax.dot_general(genotype, extended, (((0,), (0,)), ((), ())), precision=l...]
    pallas_call x0 -> x8, Pallas kernels: none -> 23.5 us  [the longest x2 11.7 us: body(): call(pair_kernel, [(width, width), (8, width)], [SMEM] + [VMEM] * 2, star...]
    all_to_all x0 -> x1, blocking collectives: none -> 16 us  [body(): lax.all_to_all(sums.reshape(2 * samp_count, row_count // 2, 2 * columns),...]
    reduce_sum x2 -> x0, other arithmetic: 11.2 us -> none  [the longest x1 5.99 us: body(): centred_sq = jnp.sum((extended - column_mean[None, :]) ** 2, axis=0)]
    all_to_all x0 -> x1, starting transfers between devices: none -> 6.75 us  [body(): packs = lax.all_to_all(pack, 'samp', 0, 0)]
  transfers between devices with their start and end apart: 5 -> 5, of which waited for: 3 -> 1; matrix products, arithmetic and copies ran while one was open for 7% -> 2% of each run, Pallas kernels for 0% -> 30%
where the time goes in v2:
time: 67.5 us; the launch traced here: 67 us
  Pallas kernels  23.5 us (35%)
  starting transfers between devices  16.4 us (24%)
  blocking collectives  16 us (24%)
  local copies, waits for them, and re-layouts  9.49 us (14%)
  waiting for transfers between devices  1.43 us (2%)
    all_to_all x1, blocking collectives, body(): lax.all_to_all(sums.reshape(2 * samp_count, row_count // 2, 2 * columns),...  16 us
    pallas_call x2, Pallas kernels, body(): call(pair_kernel, [(width, width), (8, width)], [SMEM] + [VMEM] * 2, star...  11.7 us
    unnamed x14, local copies, waits for them, and re-layouts  7.88 us
    all_to_all x1, starting transfers between devices, body(): packs = lax.all_to_all(pack, 'samp', 0, 0)  6.75 us
    ppermute x1, starting transfers between devices, body(): first = lax.ppermute(sent, 'snp', cross_pairs)  4.65 us
    ppermute x1, starting transfers between devices, body(): later = lax.ppermute(later, 'snp', cross_pairs)  4.21 us
    pallas_call x1, Pallas kernels, body(): call(own_kernel, [(width, width)], [VMEM] * 2, [pltpu.VMEM((width, width)...  3.07 us
    pallas_call x1, Pallas kernels, body(): call(far_kernel, [(samp_count, 2, row_count // 2, 2 * columns)], [SMEM] +...  2.98 us
  transfers between devices with their start and end apart: 5, of which 1 were waited for; matrix products, arithmetic and copies ran while one was open for 2% of the time, Pallas kernels for 30%

profile of v2, /device:TPU:97, one launch (start us, length us, event | category | flops | bytes accessed | tf_op | source)
XLA Modules:
  0.0 67.0 jit_solution(12335247317842433681)
XLA Ops:
  0.0 0.7 %collective-permute-start.2 = (f32[2048,512]{1,0:T(8,128)}, f32[2048,512]{1,0:T(8,128)}, u32[]{:S(2)}, u32[]{:S(2)}) collective-permute-start(f32[2048,512]{1,0:T(8,128)} %geno.11), channel_id=1, source_target_pairs={{0,1},{1,0},{2,3},{3,2},{4,5},{5,4},{6,7},{7,6},{8,9},{9,8},{10,11... | collective-permute-start | bytes 12582920 | tf_op jit(solution)/shard_map/ppermute | solution.py:281
  0.7 1.5 %constant_dynamic-slice_fusion.sent = f32[768,512]{1,0:T(8,128)S(1)} fusion(f32[2048,512]{1,0:T(8,128)} %geno.11, s32[]{:T(128)S(6)} %select_n.3), kind=kLoop, calls=%fused_computation | loop fusion | bytes 3145732 | tf_op jit(solution)/shard_map/dynamic_slice | solution.py:279
  2.2 4.6 %collective-permute-start = (f32[768,512]{1,0:T(8,128)S(1)}, f32[768,512]{1,0:T(8,128)}, u32[]{:S(2)}, u32[]{:S(2)}) collective-permute-start(f32[768,512]{1,0:T(8,128)S(1)} %constant_dynamic-slice_fusion.sent), channel_id=1, source_target_pairs={{1,2},{2,1},{3,4},{4,3},{5,6},{6,5},{7,8},{8,7},{9,10},{10,9},{11,... | collective-permute-start | bytes 4718600 | tf_op jit(solution)/shard_map/ppermute | solution.py:280
  6.9 0.1 stack.27.place
  7.0 2.2 %copy-done = f32[2048,512]{1,0:T(8,128)S(1)} copy-done((f32[2048,512]{1,0:T(8,128)S(1)}, f32[2048,512]{1,0:T(8,128)}, u32[]{:S(2)}) %copy-start) | copy-done | bytes 4194328
  9.2 0.7 copy-done.5
  9.8 0.7 copy-done.6
  10.5 2.1 %stat_kernel.1 = (f32[16,16,128]{2,1,0:T(8,128)}, f32[8,512]{1,0:T(8,128)S(1)}) custom-call(s32[6]{0:T(128)S(1)} %stack.27.place, f32[2048,512]{1,0:T(8,128)S(1)} %copy-done, s32[1,32]{1,0:T(1,128)S(1)} %bitcast.12, s32[1,32]{1,0:T(1,128)S(1)} %bitcast.13, f32[768,512]{1,0:T(8,128)S(1)} %constant_dynamic-slice_fusion.sent), custom_call_target="tpu_custom_call" | custom-call | flops 1000 | bytes 1000 | tf_op jit(solution)/shard_map/stat_kernel/pallas_call | solution.py:282
  12.6 6.8 %all-to-all-start = ((f32[16,16,128]{2,1,0:T(8,128)}), f32[16,16,128]{2,1,0:T(8,128)S(1)}, u32[]{:S(2)}, u32[]{:S(2)}) async-start(f32[16,16,128]{2,1,0:T(8,128)} %get-tuple-element.15), calls=%async_computation | async-start | bytes 262144 | tf_op jit(solution)/shard_map/all_to_all | solution.py:287
  19.3 0.0 copy-start.1
  19.4 2.2 %copy-done.1 = f32[2048,512]{1,0:T(8,128)S(1)} copy-done((f32[2048,512]{1,0:T(8,128)S(1)}, f32[2048,512]{1,0:T(8,128)}, u32[]{:S(2)}) %copy-start.1) | copy-done | bytes 4194328
  21.5 3.1 %own_kernel.1.own_products = f32[512,512]{1,0:T(8,128)S(1)} custom-call(f32[2048,512]{1,0:T(8,128)S(1)} %copy-done.1, f32[8,512]{1,0:T(8,128)S(1)} %get-tuple-element.16.means), custom_call_target="tpu_custom_call" | custom-call | flops 3221225472 | bytes 1000 | tf_op jit(solution)/shard_map/own_kernel/pallas_call | solution.py:288
  24.6 1.4 %all-to-all-done.packs = f32[16,16,128]{2,1,0:T(8,128)S(1)} async-done(((f32[16,16,128]{2,1,0:T(8,128)}), f32[16,16,128]{2,1,0:T(8,128)S(1)}, u32[]{:S(2)}, u32[]{:S(2)}) %all-to-all-start) | async-done | bytes 131104 | tf_op jit(solution)/shard_map/all_to_all | solution.py:287
  26.0 2.2 %copy-done.2 = f32[2048,512]{1,0:T(8,128)S(1)} copy-done((f32[2048,512]{1,0:T(8,128)S(1)}, f32[2048,512]{1,0:T(8,128)}, u32[]{:S(2)}) %copy-start.2) | copy-done | bytes 4194328
  28.2 0.6 combine_kernel.1
  28.8 0.0 copy-start.3
  28.9 4.2 %collective-permute-start.1 = (f32[328,512]{1,0:T(8,128)S(1)}, f32[328,512]{1,0:T(8,128)S(1)}, u32[]{:S(2)}, u32[]{:S(2)}) collective-permute-start(f32[328,512]{1,0:T(8,128)S(1)} %get-tuple-element.17), channel_id=1, source_target_pairs={{1,2},{2,1},{3,4},{4,3},{5,6},{6,5},{7,8},{8,7},{9,10},{10,9},{11,... | collective-permute-start | bytes 2015240 | tf_op jit(solution)/shard_map/ppermute | solution.py:305
  33.1 0.1 collective-permute-start.3
  33.2 3.9 %pair_kernel.2 = (f32[512,512]{1,0:T(8,128)S(1)}, f32[8,512]{1,0:T(8,128)S(1)}) custom-call(s32[6]{0:T(128)S(1)} %stack.27.place, f32[2048,512]{1,0:T(8,128)S(1)} %copy-done.2, f32[768,512]{1,0:T(8,128)} %collective-permute-done.other), custom_call_target="tpu_custom_call" | custom-call | flops 1000 | bytes 1000 | tf_op jit(solution)/shard_map/pair_kernel/pallas_call | solution.py:315
  37.1 7.9 %pair_kernel.3 = (f32[512,512]{1,0:T(8,128)S(1)}, f32[8,512]{1,0:T(8,128)S(1)}) custom-call(s32[6]{0:T(128)S(1)} %stack.27.place, f32[2048,512]{1,0:T(8,128)S(1)} %copy-done.3, f32[2048,512]{1,0:T(8,128)} %collective-permute-done.2.other), custom_call_target="tpu_custom_call" | custom-call | flops 3221225472 | bytes 1000 | tf_op jit(solution)/shard_map/pair_kernel/pallas_call | solution.py:291
  44.9 2.3 %near_kernel.1.near = f32[512,64]{1,0:T(8,128)S(1)} custom-call(s32[6]{0:T(128)S(1)} %stack.27.place, f32[512,512]{1,0:T(8,128)S(1)} %own_kernel.1.own_products, f32[8,512]{1,0:T(8,128)S(1)} %get-tuple-element.16.means, f32[512,512]{1,0:T(8,128)S(1)} %get-tuple-element.19.mate_products, f32[8,512]{1,0:T(8,128)S(1)} %get-tuple-element.20.mate_means, ...), custom_call_target="tpu_custom_call" | custom-call | flops 1000 | bytes 1000 | tf_op jit(solution)/shard_map/near_kernel/pallas_call | solution.py:307
  47.3 3.0 %far_kernel.1 = f32[16,2,16,128]{3,2,1,0:T(8,128)S(1)} custom-call(s32[6]{0:T(128)S(1)} %stack.27.place, f32[2048,512]{1,0:T(8,128)S(1)} %copy-done.3, f32[512,512]{1,0:T(8,128)S(1)} %get-tuple-element.13.products_in, f32[8,512]{1,0:T(8,128)S(1)} %get-tuple-element.14.means, f32[328,512]{1,0:T(8,128)S(1)} %collective-permute-done.1.later, ...), custom_call_target="tpu_custom_call" | custom-call | flops 1000 | bytes 1000 | tf_op jit(solution)/shard_map/far_kernel/pallas_call | solution.py:322
  50.3 16.0 %all_to_all.10.parts = f32[32,16,128]{2,1,0:T(8,128)S(1)} all-to-all(f32[32,16,128]{2,1,0:T(8,128)S(1)} %bitcast.10), channel_id=1, replica_groups={{1,2,17,18,33,34,49,50,65,66,81,82,97,98,113,114,129,130,145,146,161,16..., dimensions={0} | all-to-all | bytes 524288 | tf_op jit(solution)/shard_map/all_to_all | solution.py:332
  66.3 0.7 %last_kernel.1 = f32[32,64]{1,0:T(8,128)} custom-call(f32[32,16,128]{2,1,0:T(8,128)S(1)} %all_to_all.10.parts), custom_call_target="tpu_custom_call" | custom-call | flops 1000 | bytes 1000 | tf_op jit(solution)/shard_map/last_kernel/pallas_call | solution.py:339
  (11 shorter events, 0.0 us)
Async XLA Ops:
  0.0 37.0 %collective-permute-start.2 = (f32[2048,512]{1,0:T(8,128)}, f32[2048,512]{1,0:T(8,128)}, u32[]{:S(2)}, u32[]{:S(2)}) collective-permute-start(f32[2048,512]{1,0:T(8,128)} %geno.11), channel_id=1, source_target_pairs={{0,1},{1,0},{2,3},{3,2},{4,5},{5,4},{6,7},{7,6},{8,9},{9,8},{10,11... | collective-permute-start | bytes 12582920 | tf_op jit(solution)/shard_map/ppermute | solution.py:281
  2.2 31.0 %collective-permute-start = (f32[768,512]{1,0:T(8,128)S(1)}, f32[768,512]{1,0:T(8,128)}, u32[]{:S(2)}, u32[]{:S(2)}) collective-permute-start(f32[768,512]{1,0:T(8,128)S(1)} %constant_dynamic-slice_fusion.sent), channel_id=1, source_target_pairs={{1,2},{2,1},{3,4},{4,3},{5,6},{6,5},{7,8},{8,7},{9,10},{10,9},{11,... | collective-permute-start | bytes 4718600 | tf_op jit(solution)/shard_map/ppermute | solution.py:280
  7.0 2.2 %copy-start = (f32[2048,512]{1,0:T(8,128)S(1)}, f32[2048,512]{1,0:T(8,128)}, u32[]{:S(2)}) copy-start(f32[2048,512]{1,0:T(8,128)} %geno.11) | copy-start | bytes 12582916
  9.1 0.7 copy-start.5
  9.8 0.7 copy-start.6
  12.6 13.5 %all-to-all-start = ((f32[16,16,128]{2,1,0:T(8,128)}), f32[16,16,128]{2,1,0:T(8,128)S(1)}, u32[]{:S(2)}, u32[]{:S(2)}) async-start(f32[16,16,128]{2,1,0:T(8,128)} %get-tuple-element.15), calls=%async_computation | async-start | bytes 262144 | tf_op jit(solution)/shard_map/all_to_all | solution.py:287
  19.3 2.2 %copy-start.1 = (f32[2048,512]{1,0:T(8,128)S(1)}, f32[2048,512]{1,0:T(8,128)}, u32[]{:S(2)}) copy-start(f32[2048,512]{1,0:T(8,128)} %geno.11) | copy-start | bytes 12582916
  21.5 4.5 %copy-start.4 = (f32[512,64]{0,1:T(8,128)S(1)}, f32[512,64]{0,1:T(8,128)}, u32[]{:S(2)}) copy-start(f32[512,64]{0,1:T(8,128)} %param.5) | copy-start | bytes 393220
  26.0 2.2 %copy-start.2 = (f32[2048,512]{1,0:T(8,128)S(1)}, f32[2048,512]{1,0:T(8,128)}, u32[]{:S(2)}) copy-start(f32[2048,512]{1,0:T(8,128)} %geno.11) | copy-start | bytes 12582916
  28.8 8.2 %copy-start.3 = (f32[2048,512]{1,0:T(8,128)S(1)}, f32[2048,512]{1,0:T(8,128)}, u32[]{:S(2)}) copy-start(f32[2048,512]{1,0:T(8,128)} %geno.11) | copy-start | bytes 12582916
  28.9 18.4 %collective-permute-start.1 = (f32[328,512]{1,0:T(8,128)S(1)}, f32[328,512]{1,0:T(8,128)S(1)}, u32[]{:S(2)}, u32[]{:S(2)}) collective-permute-start(f32[328,512]{1,0:T(8,128)S(1)} %get-tuple-element.17), channel_id=1, source_target_pairs={{1,2},{2,1},{3,4},{4,3},{5,6},{6,5},{7,8},{8,7},{9,10},{10,9},{11,... | collective-permute-start | bytes 2015240 | tf_op jit(solution)/shard_map/ppermute | solution.py:305
  33.1 11.9 %collective-permute-start.3 = (f32[72,512]{1,0:T(8,128)S(1)}, f32[72,512]{1,0:T(8,128)S(1)}, u32[]{:S(2)}, u32[]{:S(2)}) collective-permute-start(f32[72,512]{1,0:T(8,128)S(1)} %get-tuple-element.18.own), channel_id=1, source_target_pairs={{0,1},{1,0},{2,3},{3,2},{4,5},{5,4},{6,7},{7,6},{8,9},{9,8},{10,11... | collective-permute-start | bytes 442376 | tf_op jit(solution)/shard_map/ppermute | solution.py:306

commit v3 on v2

v3 whole, which is shorter than its diff:
```python
import functools

import jax
import jax.numpy as jnp
from jax import lax
from jax.experimental import pallas as pl
from jax.experimental.pallas import tpu as pltpu
from jax.sharding import PartitionSpec as P

EPSILON = 1e-05
F32 = jnp.float32
BF16 = jnp.bfloat16
LANES = 128
READS = 4
VMEM = pl.BlockSpec(memory_space=pltpu.VMEM)
HBM = pl.BlockSpec(memory_space=pltpu.HBM)
ANY = pl.BlockSpec(memory_space=pl.ANY)


def split(values):
    high = values.astype(BF16)
    return high, (values - high.astype(F32)).astype(BF16)


def dot(left, right, left_dim, right_dim):
    return lax.dot_general(
        left, right, (((left_dim,), (right_dim,)), ((), ())), preferred_element_type=F32
    )


def three_dots(left, right, left_dim, right_dim):
    (left_high, left_low), (right_high, right_low) = left, right
    return (
        dot(left_high, right_high, left_dim, right_dim)
        + dot(left_high, right_low, left_dim, right_dim)
        + dot(left_low, right_high, left_dim, right_dim)
    )


def position(geno_rows):
    block = lax.axis_index("snp")
    odd = lax.rem(block, 2)
    half = geno_rows // 2
    return block, odd, odd * half, (1 - odd) * half


def column_sum(values):
    return jnp.sum(values, axis=0, keepdims=True)


def copies_in(source, begin, target, sems, pieces):
    rows = target.shape[0] // pieces
    return [
        pltpu.make_async_copy(
            source.at[pl.ds(pl.multiple_of(begin + i * rows, 8), rows)],
            target.at[pl.ds(i * rows, rows)],
            sems.at[i],
        )
        for i in range(pieces)
    ]


def start(*groups):
    for group in groups:
        for copy in group:
            copy.start()


def finish(*copies):
    for copy in copies:
        copy.wait()


def copy_kernel(geno, out, sems):
    sent_at = position(geno.shape[0])[2]
    copies = copies_in(geno, sent_at, out, sems, READS)
    start(copies)
    finish(*copies)


def stat_kernel(
    geno,
    starts,
    ends,
    sent,
    pack,
    means,
    products,
    values,
    edges,
    sems,
    edge_sems,
):
    del sent
    rows, width = values.shape
    piece = rows // READS
    copies = copies_in(geno, 0, values, sems, READS)
    edge_copies = [
        pltpu.make_async_copy(ref, edges.at[pl.ds(i, 1)], edge_sems.at[i])
        for i, ref in enumerate((starts, ends))
    ]
    start(copies, edge_copies)
    for i, copy in enumerate(copies):
        copy.wait()
        at = slice(i * piece, (i + 1) * piece)
        if i == 0:
            centre = column_sum(values[at]) / piece
        near_centre = values[at] - centre
        part, squares = column_sum(near_centre), column_sum(near_centre * near_centre)
        high, low = split(near_centre)
        product = dot(high, high * 0.5, 0, 0) + dot(high, low, 0, 0)
        if i == 0:
            total, spread = part, squares
            products[...] = product
        else:
            total, spread = total + part, spread + squares
            products[...] += product
    offset = total / rows
    mean = centre + offset
    spread = spread - rows * offset * offset
    offsets = jnp.broadcast_to(offset, (8, width))
    products[...] += products[...].T - (rows * offsets.T[:, 0:1]) * offset
    means[...] = jnp.broadcast_to(mean, means.shape)
    tiles = width // LANES
    here = edges.shape[1]
    slot = (
        lax.broadcasted_iota(jnp.int32, (tiles, LANES), 0) * (LANES // here)
        + lax.broadcasted_iota(jnp.int32, (tiles, LANES), 1) // here
    )
    mine = slot == lax.axis_index("samp")
    finish(*edge_copies)

    def spread_out(i):
        row = jnp.concatenate([edges[i : i + 1].astype(F32)] * (LANES // here), axis=1)
        return jnp.where(mine, jnp.broadcast_to(row, (tiles, LANES)), jnp.float32(0.0))

    rows_out = [
        vector[:, t * LANES : (t + 1) * LANES] for vector in (mean, spread) for t in range(tiles)
    ]
    rows_out += [spread_out(0), spread_out(1)]
    pack[...] = jnp.broadcast_to(jnp.concatenate(rows_out, axis=0)[None], pack.shape)


def combine_kernel(packs, effect, mate_means, own, *, samples_here):
    del mate_means
    count, _, _ = packs.shape
    columns, width = effect.shape
    tiles = width // LANES
    total = samples_here * count
    values = packs[...]
    means = values[:, :tiles]
    mean = jnp.sum(means, axis=0) / count
    spread = jnp.sum(values[:, tiles : 2 * tiles], axis=0)
    spread = spread + samples_here * jnp.sum((means - mean[None]) ** 2, axis=0)
    scale = lax.rsqrt(spread / total + EPSILON)
    starts = jnp.sum(values[:, 2 * tiles : 3 * tiles], axis=0)
    ends = jnp.sum(values[:, 3 * tiles :], axis=0)

    def as_row(tiled):
        return jnp.concatenate([tiled[t : t + 1] for t in range(tiles)], axis=1)

    info = jnp.concatenate(
        [as_row(mean), as_row(scale), as_row(starts), as_row(ends), jnp.zeros((4, width), F32)],
        axis=0,
    )
    own[:columns] = effect[...]
    own[columns:] = info


def in_triangle(width, reaches_right, work):
    lower, upper, every = slice(0, width // 2), slice(width // 2, width), slice(0, width)

    @pl.when(reaches_right)
    def _():
        work([(lower, lower), (upper, every)])

    @pl.when(jnp.logical_not(reaches_right))
    def _():
        work([(lower, every), (upper, upper)])


def block_dots(left, right, rows, cols):
    return three_dots([part[:, rows] for part in left], [part[:, cols] for part in right], 0, 0)


def mate_kernel(
    geno, mate, means, out, mate_means, values, mate_values, products, sems, mate_sems, out_sem
):
    rows, width = values.shape
    odd = position(rows)[1]
    half = width // 2
    writes = [
        pltpu.make_async_copy(
            products.at[pl.ds(i * half, half)], out.at[pl.ds(i * half, half)], out_sem.at[i]
        )
        for i in range(2)
    ]
    products[:half, half:] = jnp.zeros((half, half), F32)
    products[half:, :half] = jnp.zeros((half, half), F32)
    copies = copies_in(geno, 0, values, sems, READS)
    mate_copies = copies_in(mate, 0, mate_values, mate_sems, READS)
    for copy, mate_copy in zip(copies, mate_copies):
        copy.start()
        mate_copy.start()
    mean = means[0:1]
    piece = rows // READS
    centre = None
    total = None
    for i in range(READS):
        at = slice(i * piece, (i + 1) * piece)
        copies[i].wait()
        mate_copies[i].wait()
        part = column_sum(mate_values[at])
        total = part if total is None else total + part
        centre = part / piece if centre is None else centre

        def work(blocks):
            left, right = split(values[at] - mean), split(mate_values[at] - centre)
            for block_rows, block_cols in blocks:
                product = block_dots(left, right, block_rows, block_cols)
                if i == 0:
                    products[block_rows, block_cols] = product
                else:
                    products[block_rows, block_cols] += product
                if i == READS - 1:
                    writes[block_rows.start // half].start()

        in_triangle(width, odd == 0, work)
    mate_means[...] = jnp.broadcast_to(total / rows, mate_means.shape)
    finish(*writes)


def inside(first, shape, dim, starts, ends):
    index = (first + lax.broadcasted_iota(jnp.int32, shape, dim)).astype(F32)
    return (index >= starts) & (index < ends)


def near_kernel(
    geno,
    own_products,
    means,
    mate_products,
    mate_means,
    own,
    mate,
    out,
    kept,
    near_products,
    mate_sem,
    kept_sems,
    *,
    columns,
    samples_here,
    total,
):
    width = own_products.shape[0]
    block, odd, _, kept_at = position(samples_here)
    mate_copies = copies_in(mate_products, 0, near_products, mate_sem, 1)
    kept_copies = copies_in(geno, kept_at, kept, kept_sems, 2)
    start(mate_copies, kept_copies)
    info = own[columns : columns + 4]
    mean, scale = info[0:1], info[1:2]
    mate_mean, mate_scale = mate[columns : columns + 1], mate[columns + 1 : columns + 2]
    shift = means[0:1] - mean
    across = jnp.concatenate([info, shift, jnp.zeros((3, width), F32)], axis=0).T
    row_shift = samples_here * across[:, 4:5]
    row_scale = across[:, 1:2] * (1.0 / total)
    starts, ends = across[:, 2:3], across[:, 3:4]

    def part(at, cols, ref, col_shift, col_scale, block_at, source):
        centred = ref[at, cols] + row_shift[at] * col_shift[:, cols]
        first_column = block_at * width + cols.start
        keep = inside(first_column, centred.shape, 1, starts[at], ends[at])
        band = jnp.where(keep, centred * (row_scale[at] * col_scale[:, cols]), jnp.float32(0.0))
        return three_dots(split(band), split(source[:columns, cols]), 1, 1)

    every = slice(0, width)
    out[...] = part(every, every, own_products, shift, scale, block, own)
    mate_shift = mate_means[0:1] - mate_mean

    finish(*mate_copies)

    def mate_work(blocks):
        for at, cols in blocks:
            out[at] += part(
                at, cols, near_products, mate_shift, mate_scale, block + 1 - 2 * odd, mate
            )

    in_triangle(width, odd == 0, mate_work)
    finish(*kept_copies)


def cross_kernel(kept, means, across, products, cross_means, others, other_sems):
    rows, width = others.shape
    odd = position(rows)[1]
    pieces = other_sems.shape[0]
    piece = rows // pieces
    other_copies = copies_in(across, 0, others, other_sems, pieces)
    start(other_copies)
    mean = means[0:1]
    centre = None
    for i in range(pieces):
        at = slice(i * piece, (i + 1) * piece)
        other_copies[i].wait()
        part = column_sum(others[at])
        if i == 0:
            centre = part / piece
            other_sum = part
        else:
            other_sum = other_sum + part

        def work(blocks):
            left = kept[at] - mean
            total = column_sum(left)
            if i == 0:
                cross_means[0:1] = total
            else:
                cross_means[0:1] += total
            left, right = split(left), split(others[at] - centre)
            for block_rows, block_cols in blocks:
                product = block_dots(left, right, block_rows, block_cols)
                if i == 0:
                    products[block_rows, block_cols] = product
                else:
                    products[block_rows, block_cols] += product

        in_triangle(width, odd == 1, work)
    cross_means[1:2] = other_sum / rows
    cross_means[2:3] = centre
    cross_means[3:] = jnp.zeros((5, width), F32)


def far_kernel(
    products,
    means,
    cross_means,
    far,
    own,
    near,
    out,
    own_sum,
    far_sum,
    *,
    columns,
    total,
    samples_here,
):
    width = own.shape[1]
    rows = samples_here // 2
    block, odd = position(samples_here)[:2]
    info = far[columns : columns + 4]
    far_mean, far_scale = info[0:1], info[1:2]
    shift = means[0:1] - own[columns : columns + 1]
    across = jnp.concatenate(
        [own[columns : columns + 4], cross_means[0:1], shift, jnp.zeros((2, width), F32)], axis=0
    ).T
    row_scale = across[:, 1:2] * (1.0 / total)
    left_sum, row_shift = across[:, 4:5], rows * across[:, 5:6]
    centre_shift = cross_means[2:3] - far_mean
    other_shift = cross_means[1:2] - far_mean
    far_block = block + 2 * odd - 1
    count, _, piece_rows, lanes = out.shape

    def pieces(values):
        parts = values.reshape(count, 2, piece_rows, columns)
        return jnp.concatenate([parts[:, 0], parts[:, 1]], axis=-1)

    far_sum[...] = jnp.zeros_like(far_sum)

    def work(blocks):
        for at, cols in blocks:
            centred = products[at, cols] + left_sum[at] * centre_shift[:, cols]
            centred = centred + row_shift[at] * other_shift[:, cols]
            correlation = centred * (row_scale[at] * far_scale[:, cols])
            keep_own = inside(
                far_block * width + cols.start, centred.shape, 1, across[at, 2:3], across[at, 3:4]
            )
            keep_far = inside(
                block * width + at.start, centred.shape, 0, info[2:3, cols], info[3:4, cols]
            )
            own_band = jnp.where(keep_own, correlation, jnp.float32(0.0))
            far_band = jnp.where(keep_far, correlation, jnp.float32(0.0))
            own_sum[at] = near[at] + three_dots(
                split(own_band), split(far[:columns, cols]), 1, 1
            )
            far_sum[:, cols] += three_dots(split(own[:columns, at]), split(far_band), 1, 0)

    in_triangle(width, odd == 1, work)
    out[:, 1 - odd] = pieces(own_sum[...])
    out[:, odd] = pieces(far_sum[...].T)


def last_kernel(parts, out):
    total = jnp.sum(parts[...], axis=0)
    rows, columns = out.shape
    out[: rows // 2] = total[:, :columns]
    out[rows // 2 :] = total[:, columns:]


def call(kernel, shapes, specs, scratch=(), flops=1000, out_specs=None, **sizes):
    outs = [shape if hasattr(shape, "dtype") else jax.ShapeDtypeStruct(shape, F32) for shape in shapes]
    return pl.pallas_call(
        functools.partial(kernel, **sizes),
        out_shape=outs,
        in_specs=specs,
        out_specs=out_specs or [VMEM] * len(outs),
        scratch_shapes=list(scratch),
        compiler_params=pltpu.CompilerParams(vmem_limit_bytes=48 * 1024 * 1024),
        cost_estimate=pl.CostEstimate(flops=flops, bytes_accessed=1000, transcendentals=0),
        name=kernel.__name__,
    )


def body(genotype, effect, window_start, window_end):
    samp_count = lax.axis_size("samp")
    snp_count = lax.axis_size("snp")
    samples_here, width = genotype.shape
    columns = effect.shape[1]
    row_count = width // samp_count
    total = samples_here * samp_count
    half = samples_here // 2
    info_rows = columns + 8
    gram_flops = 6 * width * width * samples_here
    chip_pairs = [(i, i ^ 1) for i in range(snp_count)]
    cross = [(i, (i + 1) % snp_count) for i in range(1, snp_count, 2)]
    cross_pairs = [pair for i, j in cross[:-1] for pair in ((i, j), (j, i))]
    effect_rows = effect.T
    square = (width, width)
    whole = (samples_here, width)
    in_hbm = pltpu.with_memory_space_constraint(genotype, pltpu.HBM)
    reads = pltpu.SemaphoreType.DMA((READS,))

    sent = call(copy_kernel, [(half, width)], [HBM], [reads])(in_hbm)[0]
    across = lax.ppermute(sent, "snp", cross_pairs)
    mate = lax.ppermute(genotype, "snp", chip_pairs)
    pack, means, own_products = call(
        stat_kernel,
        [
            (samp_count, 4 * width // LANES, LANES),
            (8, width),
            square,
        ],
        [HBM, HBM, HBM, ANY],
        [
            pltpu.VMEM(whole, F32),
            pltpu.VMEM((2, row_count), jnp.int32),
            reads,
            pltpu.SemaphoreType.DMA((2,)),
        ],
    )(
        in_hbm,
        pltpu.with_memory_space_constraint(window_start[None], pltpu.HBM),
        pltpu.with_memory_space_constraint(window_end[None], pltpu.HBM),
        sent,
    )
    packs = lax.all_to_all(pack, "samp", 0, 0)
    mate_products, mate_means = call(
        mate_kernel,
        [pltpu.HBM(square, F32), (8, width)],
        [HBM, HBM, VMEM],
        [
            pltpu.VMEM(whole, F32),
            pltpu.VMEM(whole, F32),
            pltpu.VMEM(square, F32),
            reads,
            reads,
            pltpu.SemaphoreType.DMA((2,)),
        ],
        out_specs=[HBM, VMEM],
        flops=2 * gram_flops,
    )(in_hbm, pltpu.with_memory_space_constraint(mate, pltpu.HBM), means)
    own = call(
        combine_kernel,
        [(info_rows, width)],
        [VMEM] * 2 + [ANY],
        samples_here=samples_here,
    )(packs, effect_rows, mate_means)[0]
    far = lax.ppermute(own, "snp", cross_pairs)
    mate_info = lax.ppermute(own, "snp", chip_pairs)
    near, kept = call(
        near_kernel,
        [(width, columns), (half, width)],
        [HBM, VMEM, VMEM, HBM] + [VMEM] * 3,
        [pltpu.VMEM(square, F32), pltpu.SemaphoreType.DMA((1,)), pltpu.SemaphoreType.DMA((2,))],
        columns=columns,
        samples_here=samples_here,
        total=total,
    )(
        in_hbm,
        own_products,
        means,
        pltpu.with_memory_space_constraint(mate_products, pltpu.HBM),
        mate_means,
        own,
        mate_info,
    )
    cross_products, cross_means = call(
        cross_kernel,
        [square, (8, width)],
        [VMEM, VMEM, HBM],
        [pltpu.VMEM((half, width), F32), pltpu.SemaphoreType.DMA((2,))],
        flops=gram_flops,
    )(kept, means, pltpu.with_memory_space_constraint(across, pltpu.HBM))
    sums = call(
        far_kernel,
        [(samp_count, 2, row_count // 2, 2 * columns)],
        [VMEM] * 6,
        [pltpu.VMEM((width, columns), F32), pltpu.VMEM((columns, width), F32)],
        columns=columns,
        total=total,
        samples_here=samples_here,
    )(cross_products, means, cross_means, far, own, near)[0]
    groups = [[s * snp_count + i for s in range(samp_count) for i in pair] for pair in cross]
    parts = lax.all_to_all(
        sums.reshape(2 * samp_count, row_count // 2, 2 * columns),
        ("samp", "snp"),
        0,
        0,
        axis_index_groups=groups,
    )
    return call(last_kernel, [(row_count, columns)], [VMEM])(parts)[0]


def solution(mesh):
    placed = (P("samp", "snp"), P("snp", None), P(("snp", "samp")), P(("snp", "samp")))
    return jax.shard_map(
        body, mesh=mesh, in_specs=placed, out_specs=P(("snp", "samp"), None), check_vma=False
    )
```

time: 67.5 us -> 56 us (0.83)
  local copies, waits for them, and re-layouts: 9.49 us -> 0.01 us
  Pallas kernels: 23.5 us -> 21 us
  blocking collectives: 16 us -> 18.1 us
  waiting for transfers between devices: 1.43 us -> 0.15 us
    unnamed x14 -> x2, local copies, waits for them, and re-layouts: 7.88 us -> 0.01 us
    pallas_call x7, Pallas kernels: 22.8 us -> 20.3 us  [the longest x1 6.53 us: body(): call(mate_kernel, [pltpu.HBM(square, F32), (8, width)], [HBM, HBM, VMEM],...]
    all_to_all x1, blocking collectives: 16 us -> 18.1 us  [body(): lax.all_to_all(sums.reshape(2 * samp_count, row_count // 2, 2 * columns),...]
    dynamic_slice x1 -> x0, local copies, waits for them, and re-layouts: 1.53 us -> none  [body(): sent = lax.dynamic_slice_in_dim(genotype, sent_at, first_rows, 0)]
    all_to_all x1, waiting for transfers between devices: 1.42 us -> 0.14 us  [body(): packs = lax.all_to_all(pack, 'samp', 0, 0)]
  transfers between devices with their start and end apart: 5 -> 5, of which waited for: 1 -> 1; matrix products, arithmetic and copies ran while one was open for 2% -> 0% of each run, Pallas kernels for 30% -> 34%
where the time goes in v3:
time: 56 us; the launch traced here: 55.7 us
  Pallas kernels  21 us (38%)
  blocking collectives  18.1 us (32%)
  starting transfers between devices  16.3 us (29%)
    all_to_all x1, blocking collectives, body(): lax.all_to_all(sums.reshape(2 * samp_count, row_count // 2, 2 * columns),...  18.1 us
    all_to_all x1, starting transfers between devices, body(): packs = lax.all_to_all(pack, 'samp', 0, 0)  6.77 us
    pallas_call x1, Pallas kernels, body(): call(mate_kernel, [pltpu.HBM(square, F32), (8, width)], [HBM, HBM, VMEM],...  6.53 us
    pallas_call x1, Pallas kernels, body(): call(stat_kernel, [(samp_count, 4 * width // LANES, LANES), (8, width), s...  5.35 us
    ppermute x1, starting transfers between devices, body(): across = lax.ppermute(sent, 'snp', cross_pairs)  4.65 us
    ppermute x1, starting transfers between devices, body(): far = lax.ppermute(own, 'snp', cross_pairs)  4.13 us
    pallas_call x1, Pallas kernels, body(): call(cross_kernel, [square, (8, width)], [VMEM, VMEM, HBM], [pltpu.VMEM((...  3.27 us
    pallas_call x1, Pallas kernels, body(): call(near_kernel, [(width, columns), (half, width)], [HBM, VMEM, VMEM, HB...  2.05 us
  transfers between devices with their start and end apart: 5, of which 1 were waited for; matrix products, arithmetic and copies ran while one was open for 0% of the time, Pallas kernels for 34%

profile of v3, /device:TPU:97, one launch (start us, length us, event | category | flops | bytes accessed | tf_op | source)
XLA Modules:
  0.0 55.7 jit_solution(10830179233947254978)
XLA Ops:
  0.0 0.7 %collective-permute-start = (f32[2048,512]{1,0:T(8,128)}, f32[2048,512]{1,0:T(8,128)}, u32[]{:S(2)}, u32[]{:S(2)}) collective-permute-start(f32[2048,512]{1,0:T(8,128)} %geno.7), channel_id=1, source_target_pairs={{0,1},{1,0},{2,3},{3,2},{4,5},{5,4},{6,7},{7,6},{8,9},{9,8},{10,11... | collective-permute-start | bytes 12582920 | tf_op jit(solution)/shard_map/ppermute | solution.py:435
  0.7 1.5 %copy_kernel.1.sent = f32[1024,512]{1,0:T(8,128)S(1)} custom-call(f32[2048,512]{1,0:T(8,128)} %geno.7), custom_call_target="tpu_custom_call" | custom-call | flops 1000 | bytes 1000 | tf_op jit(solution)/shard_map/copy_kernel/pallas_call | solution.py:433
  2.2 4.6 %collective-permute-start.2 = (f32[1024,512]{1,0:T(8,128)S(1)}, f32[1024,512]{1,0:T(8,128)}, u32[]{:S(2)}, u32[]{:S(2)}) collective-permute-start(f32[1024,512]{1,0:T(8,128)S(1)} %copy_kernel.1.sent), channel_id=1, source_target_pairs={{1,2},{2,1},{3,4},{4,3},{5,6},{6,5},{7,8},{8,7},{9,10},{10,9},{11,... | collective-permute-start | bytes 6291464 | tf_op jit(solution)/shard_map/ppermute | solution.py:434
  6.9 5.4 %stat_kernel.1 = (f32[16,16,128]{2,1,0:T(8,128)}, f32[8,512]{1,0:T(8,128)S(1)}, f32[512,512]{1,0:T(8,128)S(1)}) custom-call(f32[2048,512]{1,0:T(8,128)} %geno.7, s32[1,32]{1,0:T(1,128)} %bitcast.6, s32[1,32]{1,0:T(1,128)} %bitcast.7, f32[1024,512]{1,0:T(8,128)S(1)} %copy_kernel.1.sent), custom_call_target="tpu_custom_call" | custom-call | flops 1000 | bytes 1000 | tf_op jit(solution)/shard_map/stat_kernel/pallas_call | solution.py:436
  12.2 6.8 %all-to-all-start = ((f32[16,16,128]{2,1,0:T(8,128)}), f32[16,16,128]{2,1,0:T(8,128)S(1)}, u32[]{:S(2)}, u32[]{:S(2)}) async-start(f32[16,16,128]{2,1,0:T(8,128)} %get-tuple-element.18), calls=%async_computation | async-start | bytes 262144 | tf_op jit(solution)/shard_map/all_to_all | solution.py:456
  19.0 0.0 collective-permute-done.mate
  19.0 0.0 copy-start
  19.0 6.5 %mate_kernel.1 = (f32[512,512]{1,0:T(8,128)}, f32[8,512]{1,0:T(8,128)S(1)}) custom-call(f32[2048,512]{1,0:T(8,128)} %geno.7, f32[2048,512]{1,0:T(8,128)} %collective-permute-done.mate, f32[8,512]{1,0:T(8,128)S(1)} %get-tuple-element.15.means), custom_call_target="tpu_custom_call" | custom-call | flops 6442450944 | bytes 1000 | tf_op jit(solution)/shard_map/mate_kernel/pallas_call | solution.py:457
  25.6 0.1 all-to-all-done.packs
  25.7 0.0 copy-done
  25.7 0.1 combine_kernel.1.own
  25.8 0.1 collective-permute-start.1
  25.9 4.1 %collective-permute-start.3 = (f32[72,512]{1,0:T(8,128)S(1)}, f32[72,512]{1,0:T(8,128)S(1)}, u32[]{:S(2)}, u32[]{:S(2)}) collective-permute-start(f32[72,512]{1,0:T(8,128)S(1)} %combine_kernel.1.own), channel_id=1, source_target_pairs={{1,2},{2,1},{3,4},{4,3},{5,6},{6,5},{7,8},{8,7},{9,10},{10,9},{11,... | collective-permute-start | bytes 442376 | tf_op jit(solution)/shard_map/ppermute | solution.py:478
  30.0 0.0 collective-permute-done.1.mate
  30.0 2.1 %near_kernel.1 = (f32[512,64]{1,0:T(8,128)S(1)}, f32[1024,512]{1,0:T(8,128)S(1)}) custom-call(f32[2048,512]{1,0:T(8,128)} %geno.7, f32[512,512]{1,0:T(8,128)S(1)} %get-tuple-element.14.own_products, f32[8,512]{1,0:T(8,128)S(1)} %get-tuple-element.15.means, f32[512,512]{1,0:T(8,128)} %get-tuple-element.16.mate_products, ...), custom_call_target="tpu_custom_call" | custom-call | flops 1000 | bytes 1000 | tf_op jit(solution)/shard_map/near_kernel/pallas_call | solution.py:480
  32.1 0.0 collective-permute-done.2.across
  32.1 3.3 %cross_kernel.1 = (f32[512,512]{1,0:T(8,128)S(1)}, f32[8,512]{1,0:T(8,128)S(1)}) custom-call(f32[1024,512]{1,0:T(8,128)S(1)} %get-tuple-element.19.kept, f32[8,512]{1,0:T(8,128)S(1)} %get-tuple-element.15.means, f32[1024,512]{1,0:T(8,128)} %collective-permute-done.2.across), custom_call_target="tpu_custom_call" | custom-call | flops 3221225472 | bytes 1000 | tf_op jit(solution)/shard_map/cross_kernel/pallas_call | solution.py:497
  35.4 0.0 collective-permute-done.3.far
  35.4 1.5 %far_kernel.1 = f32[16,2,16,128]{3,2,1,0:T(8,128)S(1)} custom-call(f32[512,512]{1,0:T(8,128)S(1)} %get-tuple-element.20.products, f32[8,512]{1,0:T(8,128)S(1)} %get-tuple-element.15.means, f32[8,512]{1,0:T(8,128)S(1)} %get-tuple-element.21.cross_means, f32[72,512]{1,0:T(8,128)S(1)} %collective-permute-done.3.far, f32[72,512]{1,0:T(8,128)S(1)} %combine_kernel.1.own, ...), custom_call_target="tpu_custom_call" | custom-call | flops 1000 | bytes 1000 | tf_op jit(solution)/shard_map/far_kernel/pallas_call | solution.py:504
  36.9 18.1 %all_to_all.10.parts = f32[32,16,128]{2,1,0:T(8,128)S(1)} all-to-all(f32[32,16,128]{2,1,0:T(8,128)S(1)} %bitcast.4), channel_id=1, replica_groups={{1,2,17,18,33,34,49,50,65,66,81,82,97,98,113,114,129,130,145,146,161,16..., dimensions={0} | all-to-all | bytes 524288 | tf_op jit(solution)/shard_map/all_to_all | solution.py:514
  54.9 0.7 %last_kernel.1 = f32[32,64]{1,0:T(8,128)} custom-call(f32[32,16,128]{2,1,0:T(8,128)S(1)} %all_to_all.10.parts), custom_call_target="tpu_custom_call" | custom-call | flops 1000 | bytes 1000 | tf_op jit(solution)/shard_map/last_kernel/pallas_call | solution.py:521
Async XLA Ops:
  0.0 19.0 %collective-permute-start = (f32[2048,512]{1,0:T(8,128)}, f32[2048,512]{1,0:T(8,128)}, u32[]{:S(2)}, u32[]{:S(2)}) collective-permute-start(f32[2048,512]{1,0:T(8,128)} %geno.7), channel_id=1, source_target_pairs={{0,1},{1,0},{2,3},{3,2},{4,5},{5,4},{6,7},{7,6},{8,9},{9,8},{10,11... | collective-permute-start | bytes 12582920 | tf_op jit(solution)/shard_map/ppermute | solution.py:435
  2.2 29.9 %collective-permute-start.2 = (f32[1024,512]{1,0:T(8,128)S(1)}, f32[1024,512]{1,0:T(8,128)}, u32[]{:S(2)}, u32[]{:S(2)}) collective-permute-start(f32[1024,512]{1,0:T(8,128)S(1)} %copy_kernel.1.sent), channel_id=1, source_target_pairs={{1,2},{2,1},{3,4},{4,3},{5,6},{6,5},{7,8},{8,7},{9,10},{10,9},{11,... | collective-permute-start | bytes 6291464 | tf_op jit(solution)/shard_map/ppermute | solution.py:434
  12.2 13.5 %all-to-all-start = ((f32[16,16,128]{2,1,0:T(8,128)}), f32[16,16,128]{2,1,0:T(8,128)S(1)}, u32[]{:S(2)}, u32[]{:S(2)}) async-start(f32[16,16,128]{2,1,0:T(8,128)} %get-tuple-element.18), calls=%async_computation | async-start | bytes 262144 | tf_op jit(solution)/shard_map/all_to_all | solution.py:456
  19.0 6.7 %copy-start = (f32[512,64]{0,1:T(8,128)S(1)}, f32[512,64]{0,1:T(8,128)}, u32[]{:S(2)}) copy-start(f32[512,64]{0,1:T(8,128)} %param.5) | copy-start | bytes 393220
  25.8 4.2 %collective-permute-start.1 = (f32[72,512]{1,0:T(8,128)S(1)}, f32[72,512]{1,0:T(8,128)S(1)}, u32[]{:S(2)}, u32[]{:S(2)}) collective-permute-start(f32[72,512]{1,0:T(8,128)S(1)} %combine_kernel.1.own), channel_id=1, source_target_pairs={{0,1},{1,0},{2,3},{3,2},{4,5},{5,4},{6,7},{7,6},{8,9},{9,8},{10,11... | collective-permute-start | bytes 442376 | tf_op jit(solution)/shard_map/ppermute | solution.py:479
  25.9 9.5 %collective-permute-start.3 = (f32[72,512]{1,0:T(8,128)S(1)}, f32[72,512]{1,0:T(8,128)S(1)}, u32[]{:S(2)}, u32[]{:S(2)}) collective-permute-start(f32[72,512]{1,0:T(8,128)S(1)} %combine_kernel.1.own), channel_id=1, source_target_pairs={{1,2},{2,1},{3,4},{4,3},{5,6},{6,5},{7,8},{8,7},{9,10},{10,9},{11,... | collective-permute-start | bytes 442376 | tf_op jit(solution)/shard_map/ppermute | solution.py:478

commit v4 on v3

v4 whole, which is shorter than its diff:
```python
import functools

import jax
import jax.numpy as jnp
from jax import lax
from jax.experimental import pallas as pl
from jax.experimental.pallas import tpu as pltpu
from jax.sharding import PartitionSpec as P

EPSILON = 1e-05
F32 = jnp.float32
BF16 = jnp.bfloat16
LANES = 128
READS = 4
FAR_READS = 2
LAST_ROWS = 64
VMEM = pl.BlockSpec(memory_space=pltpu.VMEM)
HBM = pl.BlockSpec(memory_space=pltpu.HBM)
ANY = pl.BlockSpec(memory_space=pl.ANY)


def split(values):
    high = values.astype(BF16)
    return high, (values - high.astype(F32)).astype(BF16)


def dot(left, right, left_dim, right_dim):
    return lax.dot_general(
        left, right, (((left_dim,), (right_dim,)), ((), ())), preferred_element_type=F32
    )


def three_dots(left, right, left_dim, right_dim):
    (left_high, left_low), (right_high, right_low) = left, right
    return (
        dot(left_high, right_high, left_dim, right_dim)
        + dot(left_high, right_low, left_dim, right_dim)
        + dot(left_low, right_high, left_dim, right_dim)
    )


def position(geno_rows):
    block = lax.axis_index("snp")
    odd = lax.rem(block, 2)
    half = geno_rows // 2
    return block, odd, odd * half, (1 - odd) * half


def column_sum(values):
    return jnp.sum(values, axis=0, keepdims=True)


def copies_in(source, begin, target, sems, pieces):
    rows = target.shape[0] // pieces
    return [
        pltpu.make_async_copy(
            source.at[pl.ds(pl.multiple_of(begin + i * rows, 8), rows)],
            target.at[pl.ds(i * rows, rows)],
            sems.at[i],
        )
        for i in range(pieces)
    ]


def start(*groups):
    for group in groups:
        for copy in group:
            copy.start()


def finish(*copies):
    for copy in copies:
        copy.wait()


def copy_kernel(geno, out, sems):
    sent_at = position(geno.shape[0])[2]
    copies = copies_in(geno, sent_at, out, sems, READS)
    start(copies)
    finish(*copies)


def stat_kernel(
    geno,
    starts,
    ends,
    sent,
    pack,
    means,
    products,
    values,
    edges,
    sems,
    edge_sems,
):
    del sent
    rows, width = values.shape
    piece = rows // READS
    copies = copies_in(geno, 0, values, sems, READS)
    edge_copies = [
        pltpu.make_async_copy(ref, edges.at[pl.ds(i, 1)], edge_sems.at[i])
        for i, ref in enumerate((starts, ends))
    ]
    start(copies, edge_copies)
    for i, copy in enumerate(copies):
        copy.wait()
        at = slice(i * piece, (i + 1) * piece)
        if i == 0:
            centre = column_sum(values[at]) / piece
        near_centre = values[at] - centre
        part, squares = column_sum(near_centre), column_sum(near_centre * near_centre)
        high, low = split(near_centre)
        product = dot(high, high * 0.5, 0, 0) + dot(high, low, 0, 0)
        if i == 0:
            total, spread = part, squares
            products[...] = product
        else:
            total, spread = total + part, spread + squares
            products[...] += product
    offset = total / rows
    mean = centre + offset
    spread = spread - rows * offset * offset
    means[...] = jnp.concatenate([mean, offset, jnp.zeros((6, width), F32)], axis=0)
    tiles = width // LANES
    here = edges.shape[1]
    slot = (
        lax.broadcasted_iota(jnp.int32, (tiles, LANES), 0) * (LANES // here)
        + lax.broadcasted_iota(jnp.int32, (tiles, LANES), 1) // here
    )
    mine = slot == lax.axis_index("samp")
    finish(*edge_copies)

    def spread_out(i):
        row = jnp.concatenate([edges[i : i + 1].astype(F32)] * (LANES // here), axis=1)
        return jnp.where(mine, jnp.broadcast_to(row, (tiles, LANES)), jnp.float32(0.0))

    rows_out = [
        vector[:, t * LANES : (t + 1) * LANES] for vector in (mean, spread) for t in range(tiles)
    ]
    rows_out += [spread_out(0), spread_out(1)]
    pack[...] = jnp.broadcast_to(jnp.concatenate(rows_out, axis=0)[None], pack.shape)


def combine_kernel(packs, effect, sent_last, later, own, *, samples_here):
    count, _, _ = packs.shape
    columns, width = effect.shape
    tiles = width // LANES
    total = samples_here * count
    values = packs[...]
    means = values[:, :tiles]
    mean = jnp.sum(means, axis=0) / count
    spread = jnp.sum(values[:, tiles : 2 * tiles], axis=0)
    spread = spread + samples_here * jnp.sum((means - mean[None]) ** 2, axis=0)
    scale = lax.rsqrt(spread / total + EPSILON)
    starts = jnp.sum(values[:, 2 * tiles : 3 * tiles], axis=0)
    ends = jnp.sum(values[:, 3 * tiles :], axis=0)

    def as_row(tiled):
        return jnp.concatenate([tiled[t : t + 1] for t in range(tiles)], axis=1)

    scale_row = as_row(scale)
    info = jnp.concatenate(
        [as_row(mean), scale_row, as_row(starts), as_row(ends), jnp.zeros((4, width), F32)],
        axis=0,
    )
    scaled = effect[...] * scale_row
    own[:columns] = scaled
    own[columns:] = info
    rows = sent_last.shape[0]
    later[:rows] = sent_last[...]
    later[rows : rows + columns] = scaled
    later[rows + columns :] = info


def in_triangle(width, reaches_right, work):
    lower, upper, every = slice(0, width // 2), slice(width // 2, width), slice(0, width)

    @pl.when(reaches_right)
    def _():
        work([(lower, lower), (upper, every)], True)

    @pl.when(jnp.logical_not(reaches_right))
    def _():
        work([(lower, every), (upper, upper)], False)


def block_dots(left, right, rows, cols):
    return three_dots([part[:, rows] for part in left], [part[:, cols] for part in right], 0, 0)


def mate_kernel(
    geno,
    mate,
    means,
    half_products,
    products,
    mate_means,
    own_out,
    sent_last,
    values,
    mate_values,
    own_products,
    sems,
    mate_sems,
    out_sem,
):
    rows, width = values.shape
    _, odd, sent_at, _ = position(rows)
    last_at = pl.multiple_of(sent_at + rows // 2 - LAST_ROWS, 8)
    copies = copies_in(geno, 0, values, sems, READS)
    mate_copies = copies_in(mate, 0, mate_values, mate_sems, READS)
    for copy, mate_copy in zip(copies, mate_copies):
        copy.start()
        mate_copy.start()
    mean, offset = means[0:1], means[1:2]
    own_products[...] = (
        half_products[...]
        + half_products[...].T
        - (rows * jnp.broadcast_to(offset, (8, width)).T[:, 0:1]) * offset
    )
    write = pltpu.make_async_copy(own_products, own_out, out_sem.at[0])
    write.start()
    piece = rows // READS
    centre = None
    total = None
    for i in range(READS):
        at = slice(i * piece, (i + 1) * piece)
        copies[i].wait()
        mate_copies[i].wait()
        part = column_sum(mate_values[at])
        total = part if total is None else total + part
        centre = part / piece if centre is None else centre

        def work(blocks, right_side):
            left, right = split(values[at] - mean), split(mate_values[at] - centre)
            for block_rows, block_cols in blocks:
                product = block_dots(left, right, block_rows, block_cols)
                if i == 0:
                    products[block_rows, block_cols] = product
                else:
                    products[block_rows, block_cols] += product

        in_triangle(width, odd == 0, work)
    mate_means[...] = jnp.broadcast_to(total / rows, mate_means.shape)
    sent_last[...] = values[pl.ds(last_at, LAST_ROWS), :]
    write.wait()


def index_of(first, shape, dim):
    return (first + lax.broadcasted_iota(jnp.int32, shape, dim)).astype(F32)


def band_dot(keep, centred, source, cols, columns):
    band = jnp.where(keep, centred, jnp.float32(0.0))
    return three_dots(split(band), split(source[:columns, cols]), 1, 1)


def near_kernel(
    geno, means, mate_products, mate_means, own, mate, out, kept, kept_sems, *, columns, samples_here
):
    width = mate_products.shape[0]
    block, odd, _, kept_at = position(samples_here)
    kept_copies = copies_in(geno, kept_at, kept, kept_sems, 2)
    start(kept_copies)
    info = own[columns : columns + 4]
    shift = means[0:1] - info[0:1]
    by_row = jnp.concatenate([info, shift, jnp.zeros((3, width), F32)], axis=0).T
    row_shift = samples_here * by_row[:, 4:5]
    starts, ends = by_row[:, 2:3], by_row[:, 3:4]
    mate_shift = mate_means[0:1] - mate[columns : columns + 1]
    mate_block = block + 1 - 2 * odd

    def mate_work(blocks, right_side):
        for at, cols in blocks:
            centred = mate_products[at, cols] + row_shift[at] * mate_shift[:, cols]
            index = index_of(mate_block * width + cols.start, (1, centred.shape[1]), 1)
            keep = index < ends[at] if right_side else index >= starts[at]
            out[at] = band_dot(keep, centred, mate, cols, columns)

    in_triangle(width, odd == 0, mate_work)
    finish(*kept_copies)


def cross_kernel(
    kept,
    means,
    across,
    own_products,
    own,
    near,
    products,
    cross_means,
    near_sum,
    others,
    sems,
    *,
    columns,
    samples_here,
):
    rows, width = others.shape
    block, odd = position(rows)[:2]
    pieces = sems.shape[0]
    piece = rows // pieces
    copies = copies_in(across, 0, others, sems, pieces)
    start(copies)
    mean = means[0:1]
    info = own[columns : columns + 4]
    shift = mean - info[0:1]
    by_row = jnp.concatenate([info, shift, jnp.zeros((3, width), F32)], axis=0).T
    centred = own_products[...] + (samples_here * by_row[:, 4:5]) * shift
    index = index_of(block * width, (1, width), 1)
    keep = (index >= by_row[:, 2:3]) & (index < by_row[:, 3:4])
    near_sum[...] = near[...] + band_dot(keep, centred, own, slice(0, width), columns)
    centre = None
    for i, copy in enumerate(copies):
        copy.wait()
        at = slice(i * piece, (i + 1) * piece)
        part = column_sum(others[at])
        other_sum = part if i == 0 else other_sum + part
        centre = part / piece if i == 0 else centre

        def work(blocks, right_side):
            left = kept[at] - mean
            total = column_sum(left)
            if i == 0:
                cross_means[0:1] = total
            else:
                cross_means[0:1] += total
            left, right = split(left), split(others[at] - centre)
            for block_rows, block_cols in blocks:
                product = block_dots(left, right, block_rows, block_cols)
                if i == 0:
                    products[block_rows, block_cols] = product
                else:
                    products[block_rows, block_cols] += product

        in_triangle(width, odd == 1, work)
    cross_means[1:2] = other_sum / rows
    cross_means[2:3] = centre
    cross_means[3:] = jnp.zeros((5, width), F32)


def far_kernel(
    kept,
    products,
    means,
    cross_means,
    later,
    own,
    near,
    out,
    own_sum,
    far_sum,
    *,
    columns,
    total,
):
    half, width = kept.shape
    rows = later.shape[0] - own.shape[0]
    first_rows = half - rows
    block, odd = position(half)[:2]
    mean = own[columns : columns + 1]
    info = later[rows + columns : rows + columns + 4]
    far_mean, far_scale = info[0:1], info[1:2]
    shift = means[0:1] - mean
    by_row = jnp.concatenate(
        [own[columns : columns + 4], cross_means[0:1], shift, jnp.zeros((2, width), F32)], axis=0
    ).T
    row_scale = by_row[:, 1:2] * (1.0 / total)
    left_sum, row_shift = by_row[:, 4:5], first_rows * by_row[:, 5:6]
    centre_shift = cross_means[2:3] - far_mean
    other_shift = cross_means[1:2] - far_mean
    far_block = block + 2 * odd - 1
    count, _, piece_rows, lanes = out.shape

    def pieces_of(values):
        parts = values.reshape(count, 2, piece_rows, columns)
        return jnp.concatenate([parts[:, 0], parts[:, 1]], axis=-1)

    far_sum[...] = jnp.zeros_like(far_sum)

    def work(blocks, right_side):
        left, right = split(kept[first_rows:] - mean), split(later[:rows] - far_mean)
        for at, cols in blocks:
            centred = products[at, cols] + block_dots(left, right, at, cols)
            centred = centred + left_sum[at] * centre_shift[:, cols]
            centred = centred + row_shift[at] * other_shift[:, cols]
            row_index = index_of(block * width + at.start, (centred.shape[0], 1), 0)
            col_index = index_of(far_block * width + cols.start, (1, centred.shape[1]), 1)
            if right_side:
                keep_own = col_index < by_row[at, 3:4]
                keep_far = row_index >= info[2:3, cols]
            else:
                keep_own = col_index >= by_row[at, 2:3]
                keep_far = row_index < info[3:4, cols]
            own_sum[at] = near[at] + band_dot(
                keep_own, centred, later[rows : rows + columns], cols, columns
            )
            far_band = jnp.where(keep_far, centred, jnp.float32(0.0))
            far_sum[:, cols] += three_dots(split(own[:columns, at]), split(far_band), 1, 0)

    in_triangle(width, odd == 1, work)
    out[:, 1 - odd] = pieces_of(own_sum[...] * row_scale)
    out[:, odd] = pieces_of((far_sum[...] * (far_scale * (1.0 / total))).T)


def last_kernel(parts, out):
    total = jnp.sum(parts[...], axis=0)
    rows, columns = out.shape
    out[: rows // 2] = total[:, :columns]
    out[rows // 2 :] = total[:, columns:]


def call(kernel, shapes, specs, scratch=(), flops=1000, out_specs=None, aliases=None, **sizes):
    outs = [shape if hasattr(shape, "dtype") else jax.ShapeDtypeStruct(shape, F32) for shape in shapes]
    return pl.pallas_call(
        functools.partial(kernel, **sizes),
        out_shape=outs,
        in_specs=specs,
        out_specs=out_specs or [VMEM] * len(outs),
        scratch_shapes=list(scratch),
        input_output_aliases=aliases or {},
        compiler_params=pltpu.CompilerParams(vmem_limit_bytes=48 * 1024 * 1024),
        cost_estimate=pl.CostEstimate(flops=flops, bytes_accessed=1000, transcendentals=0),
        name=kernel.__name__,
    )


def body(genotype, effect, window_start, window_end):
    samp_count = lax.axis_size("samp")
    snp_count = lax.axis_size("snp")
    samples_here, width = genotype.shape
    columns = effect.shape[1]
    row_count = width // samp_count
    total = samples_here * samp_count
    half = samples_here // 2
    info_rows = columns + 8
    gram_flops = 6 * width * width * samples_here
    chip_pairs = [(i, i ^ 1) for i in range(snp_count)]
    cross = [(i, (i + 1) % snp_count) for i in range(1, snp_count, 2)]
    cross_pairs = [pair for i, j in cross[:-1] for pair in ((i, j), (j, i))]
    effect_rows = effect.T
    square = (width, width)
    whole = (samples_here, width)
    in_hbm = pltpu.with_memory_space_constraint(genotype, pltpu.HBM)
    reads = pltpu.SemaphoreType.DMA((READS,))

    sent = call(copy_kernel, [(half - LAST_ROWS, width)], [HBM], [reads])(in_hbm)[0]
    across = lax.ppermute(sent, "snp", cross_pairs)
    mate = lax.ppermute(genotype, "snp", chip_pairs)
    pack, means, half_products = call(
        stat_kernel,
        [
            (samp_count, 4 * width // LANES, LANES),
            (8, width),
            square,
        ],
        [HBM, HBM, HBM, ANY],
        [
            pltpu.VMEM(whole, F32),
            pltpu.VMEM((2, row_count), jnp.int32),
            reads,
            pltpu.SemaphoreType.DMA((2,)),
        ],
    )(
        in_hbm,
        pltpu.with_memory_space_constraint(window_start[None], pltpu.HBM),
        pltpu.with_memory_space_constraint(window_end[None], pltpu.HBM),
        sent,
    )
    packs = lax.all_to_all(pack, "samp", 0, 0)
    mate_products, mate_means, own_products, sent_last = call(
        mate_kernel,
        [square, (8, width), pltpu.HBM(square, F32), (LAST_ROWS, width)],
        [HBM, HBM, VMEM, VMEM],
        [
            pltpu.VMEM(whole, F32),
            pltpu.VMEM(whole, F32),
            pltpu.VMEM(square, F32),
            reads,
            reads,
            pltpu.SemaphoreType.DMA((1,)),
        ],
        out_specs=[VMEM, VMEM, HBM, VMEM],
        flops=2 * gram_flops,
        aliases={3: 0},
    )(in_hbm, pltpu.with_memory_space_constraint(mate, pltpu.HBM), means, half_products)
    later, own = call(
        combine_kernel,
        [(LAST_ROWS + info_rows, width), (info_rows, width)],
        [VMEM] * 3,
        samples_here=samples_here,
    )(packs, effect_rows, sent_last)
    far = lax.ppermute(later, "snp", cross_pairs)
    mate_info = lax.ppermute(own, "snp", chip_pairs)
    near, kept = call(
        near_kernel,
        [(width, columns), (half, width)],
        [HBM] + [VMEM] * 5,
        [pltpu.SemaphoreType.DMA((2,))],
        columns=columns,
        samples_here=samples_here,
    )(in_hbm, means, mate_products, mate_means, own, mate_info)
    cross_products, cross_means, near = call(
        cross_kernel,
        [square, (8, width), (width, columns)],
        [VMEM, VMEM, HBM] + [VMEM] * 3,
        [pltpu.VMEM((half - LAST_ROWS, width), F32), pltpu.SemaphoreType.DMA((FAR_READS,))],
        columns=columns,
        samples_here=samples_here,
        flops=gram_flops,
    )(kept, means, pltpu.with_memory_space_constraint(across, pltpu.HBM), own_products, own, near)
    sums = call(
        far_kernel,
        [(samp_count, 2, row_count // 2, 2 * columns)],
        [VMEM] * 7,
        [pltpu.VMEM((width, columns), F32), pltpu.VMEM((columns, width), F32)],
        columns=columns,
        total=total,
    )(kept, cross_products, means, cross_means, far, own, near)[0]
    groups = [[s * snp_count + i for s in range(samp_count) for i in pair] for pair in cross]
    parts = lax.all_to_all(
        sums.reshape(2 * samp_count, row_count // 2, 2 * columns),
        ("samp", "snp"),
        0,
        0,
        axis_index_groups=groups,
    )
    return call(last_kernel, [(row_count, columns)], [VMEM])(parts)[0]


def solution(mesh):
    placed = (P("samp", "snp"), P("snp", None), P(("snp", "samp")), P(("snp", "samp")))
    return jax.shard_map(
        body, mesh=mesh, in_specs=placed, out_specs=P(("snp", "samp"), None), check_vma=False
    )
```

time: 56 us -> 55 us (0.982)
  blocking collectives: 18.1 us -> 17.1 us
  waiting for transfers between devices: 0.15 us -> 1.06 us
  Pallas kernels: 21 us -> 20.1 us
    pallas_call x5, Pallas kernels: 13.5 us -> 12.1 us  [the longest x1 5.67 us: body(): call(mate_kernel, [square, (8, width), pltpu.HBM(square, F32), (LAST_ROWS...]
    all_to_all x1, blocking collectives: 18.1 us -> 17.1 us  [body(): lax.all_to_all(sums.reshape(2 * samp_count, row_count // 2, 2 * columns),...]
    all_to_all x1, waiting for transfers between devices: 0.14 us -> 0.99 us  [body(): packs = lax.all_to_all(pack, 'samp', 0, 0)]
    pallas_call x1, Pallas kernels: 1.48 us -> 2.18 us  [body(): call(far_kernel, [(samp_count, 2, row_count // 2, 2 * columns)], [VMEM] *...]
  transfers between devices with their start and end apart: 5 -> 5, of which waited for: 1 -> 2; matrix products, arithmetic and copies ran while one was open for 0% -> 0% of each run, Pallas kernels for 34% -> 31%
where the time goes in v4:
time: 55 us; the launch traced here: 54.7 us
  Pallas kernels  20.1 us (37%)
  blocking collectives  17.1 us (31%)
  starting transfers between devices  16.1 us (29%)
  waiting for transfers between devices  1.06 us (2%)
    all_to_all x1, blocking collectives, body(): lax.all_to_all(sums.reshape(2 * samp_count, row_count // 2, 2 * columns),...  17.1 us
    all_to_all x1, starting transfers between devices, body(): packs = lax.all_to_all(pack, 'samp', 0, 0)  6.77 us
    pallas_call x1, Pallas kernels, body(): call(mate_kernel, [square, (8, width), pltpu.HBM(square, F32), (LAST_ROWS...  5.67 us
    pallas_call x1, Pallas kernels, body(): call(stat_kernel, [(samp_count, 4 * width // LANES, LANES), (8, width), s...  5.1 us
    ppermute x1, starting transfers between devices, body(): across = lax.ppermute(sent, 'snp', cross_pairs)  4.65 us
    ppermute x1, starting transfers between devices, body(): far = lax.ppermute(later, 'snp', cross_pairs)  3.95 us
    pallas_call x1, Pallas kernels, body(): call(cross_kernel, [square, (8, width), (width, columns)], [VMEM, VMEM, H...  3.19 us
    pallas_call x1, Pallas kernels, body(): call(far_kernel, [(samp_count, 2, row_count // 2, 2 * columns)], [VMEM] *...  2.18 us
  transfers between devices with their start and end apart: 5, of which 2 were waited for; matrix products, arithmetic and copies ran while one was open for 0% of the time, Pallas kernels for 31%

profile of v4, /device:TPU:97, one launch (start us, length us, event | category | flops | bytes accessed | tf_op | source)
XLA Modules:
  0.0 54.7 jit_solution(5042940352031754495)
XLA Ops:
  0.0 0.7 %collective-permute-start = (f32[2048,512]{1,0:T(8,128)}, f32[2048,512]{1,0:T(8,128)}, u32[]{:S(2)}, u32[]{:S(2)}) collective-permute-start(f32[2048,512]{1,0:T(8,128)} %geno.7), channel_id=1, source_target_pairs={{0,1},{1,0},{2,3},{3,2},{4,5},{5,4},{6,7},{7,6},{8,9},{9,8},{10,11... | collective-permute-start | bytes 12582920 | tf_op jit(solution)/shard_map/ppermute | solution.py:450
  0.7 1.5 %copy_kernel.1.sent = f32[960,512]{1,0:T(8,128)S(1)} custom-call(f32[2048,512]{1,0:T(8,128)} %geno.7), custom_call_target="tpu_custom_call" | custom-call | flops 1000 | bytes 1000 | tf_op jit(solution)/shard_map/copy_kernel/pallas_call | solution.py:448
  2.2 4.6 %collective-permute-start.2 = (f32[960,512]{1,0:T(8,128)S(1)}, f32[960,512]{1,0:T(8,128)}, u32[]{:S(2)}, u32[]{:S(2)}) collective-permute-start(f32[960,512]{1,0:T(8,128)S(1)} %copy_kernel.1.sent), channel_id=1, source_target_pairs={{1,2},{2,1},{3,4},{4,3},{5,6},{6,5},{7,8},{8,7},{9,10},{10,9},{11,... | collective-permute-start | bytes 5898248 | tf_op jit(solution)/shard_map/ppermute | solution.py:449
  6.8 5.1 %stat_kernel.1 = (f32[16,16,128]{2,1,0:T(8,128)}, f32[8,512]{1,0:T(8,128)S(1)}, f32[512,512]{1,0:T(8,128)S(1)}) custom-call(f32[2048,512]{1,0:T(8,128)} %geno.7, s32[1,32]{1,0:T(1,128)} %bitcast.6, s32[1,32]{1,0:T(1,128)} %bitcast.7, f32[960,512]{1,0:T(8,128)S(1)} %copy_kernel.1.sent), custom_call_target="tpu_custom_call" | custom-call | flops 1000 | bytes 1000 | tf_op jit(solution)/shard_map/stat_kernel/pallas_call | solution.py:451
  12.0 6.8 %all-to-all-start = ((f32[16,16,128]{2,1,0:T(8,128)}), f32[16,16,128]{2,1,0:T(8,128)S(1)}, u32[]{:S(2)}, u32[]{:S(2)}) async-start(f32[16,16,128]{2,1,0:T(8,128)} %get-tuple-element.23), calls=%async_computation | async-start | bytes 262144 | tf_op jit(solution)/shard_map/all_to_all | solution.py:471
  18.7 0.0 collective-permute-done.mate
  18.7 0.0 copy-start
  18.8 5.7 %mate_kernel.1 = (f32[512,512]{1,0:T(8,128)S(1)}, f32[8,512]{1,0:T(8,128)S(1)}, f32[512,512]{1,0:T(8,128)}, f32[64,512]{1,0:T(8,128)S(1)}) custom-call(f32[2048,512]{1,0:T(8,128)} %geno.7, f32[2048,512]{1,0:T(8,128)} %collective-permute-done.mate, f32[8,512]{1,0:T(8,128)S(1)} %get-tuple-element.19.means, ...), custom_call_target="tpu_custom_call", output_to_operand_aliasing={{0}: (3, {})} | custom-call | flops 6442450944 | bytes 1000 | tf_op jit(solution)/shard_map/mate_kernel/pallas_call | solution.py:472
  24.4 1.0 %all-to-all-done.packs = f32[16,16,128]{2,1,0:T(8,128)S(1)} async-done(((f32[16,16,128]{2,1,0:T(8,128)}), f32[16,16,128]{2,1,0:T(8,128)S(1)}, u32[]{:S(2)}, u32[]{:S(2)}) %all-to-all-start) | async-done | bytes 131104 | tf_op jit(solution)/shard_map/all_to_all | solution.py:471
  25.4 0.0 copy-done
  25.4 0.1 combine_kernel.1
  25.5 0.1 collective-permute-start.1
  25.6 3.9 %collective-permute-start.3 = (f32[136,512]{1,0:T(8,128)S(1)}, f32[136,512]{1,0:T(8,128)S(1)}, u32[]{:S(2)}, u32[]{:S(2)}) collective-permute-start(f32[136,512]{1,0:T(8,128)S(1)} %get-tuple-element.31), channel_id=1, source_target_pairs={{1,2},{2,1},{3,4},{4,3},{5,6},{6,5},{7,8},{8,7},{9,10},{10,9},{11,... | collective-permute-start | bytes 835592 | tf_op jit(solution)/shard_map/ppermute | solution.py:494
  29.6 0.0 collective-permute-done.1.mate
  29.6 0.0 copy-start.1
  29.6 1.7 %near_kernel.1 = (f32[512,64]{1,0:T(8,128)S(1)}, f32[1024,512]{1,0:T(8,128)S(1)}) custom-call(f32[2048,512]{1,0:T(8,128)} %geno.7, f32[8,512]{1,0:T(8,128)S(1)} %get-tuple-element.19.means, f32[512,512]{1,0:T(8,128)S(1)} %get-tuple-element.21.mate_products, f32[8,512]{1,0:T(8,128)S(1)} %get-tuple-element.22.mate_means, f32[72,512]{1,0:T(8,128)S(1)} %get-tuple-element.25.own, ...), custom_call_target="tpu_custom_call" | custom-call | flops 1000 | bytes 1000 | tf_op jit(solution)/shard_map/near_kernel/pallas_call | solution.py:496
  31.2 0.0 collective-permute-done.2.across
  31.3 0.2 copy-done.1
  31.4 3.2 %cross_kernel.1 = (f32[512,512]{1,0:T(8,128)S(1)}, f32[8,512]{1,0:T(8,128)S(1)}, f32[512,64]{1,0:T(8,128)S(1)}) custom-call(f32[1024,512]{1,0:T(8,128)S(1)} %get-tuple-element.26.kept, f32[8,512]{1,0:T(8,128)S(1)} %get-tuple-element.19.means, f32[960,512]{1,0:T(8,128)} %collective-permute-done.2.across, f32[512,512]{1,0:T(8,128)S(1)} %copy-done.1, ...), custom_call_target="tpu_custom_call" | custom-call | flops 3221225472 | bytes 1000 | tf_op jit(solution)/shard_map/cross_kernel/pallas_call | solution.py:504
  34.6 0.1 collective-permute-done.3.later
  34.7 2.2 %far_kernel.1 = f32[16,2,16,128]{3,2,1,0:T(8,128)S(1)} custom-call(f32[1024,512]{1,0:T(8,128)S(1)} %get-tuple-element.26.kept, f32[512,512]{1,0:T(8,128)S(1)} %get-tuple-element.29.products, f32[8,512]{1,0:T(8,128)S(1)} %get-tuple-element.19.means, f32[8,512]{1,0:T(8,128)S(1)} %get-tuple-element.30.cross_means, f32[136,512]{1,0:T(8,128)S(1)} %collective-permute-done.3.later, ...), custom_call_target="tpu_custom_call" | custom-call | flops 1000 | bytes 1000 | tf_op jit(solution)/shard_map/far_kernel/pallas_call | solution.py:513
  36.9 17.1 %all_to_all.10.parts = f32[32,16,128]{2,1,0:T(8,128)S(1)} all-to-all(f32[32,16,128]{2,1,0:T(8,128)S(1)} %bitcast.4), channel_id=1, replica_groups={{1,2,17,18,33,34,49,50,65,66,81,82,97,98,113,114,129,130,145,146,161,16..., dimensions={0} | all-to-all | bytes 524288 | tf_op jit(solution)/shard_map/all_to_all | solution.py:522
  54.0 0.7 %last_kernel.1 = f32[32,64]{1,0:T(8,128)} custom-call(f32[32,16,128]{2,1,0:T(8,128)S(1)} %all_to_all.10.parts), custom_call_target="tpu_custom_call" | custom-call | flops 1000 | bytes 1000 | tf_op jit(solution)/shard_map/last_kernel/pallas_call | solution.py:529
Async XLA Ops:
  0.0 18.7 %collective-permute-start = (f32[2048,512]{1,0:T(8,128)}, f32[2048,512]{1,0:T(8,128)}, u32[]{:S(2)}, u32[]{:S(2)}) collective-permute-start(f32[2048,512]{1,0:T(8,128)} %geno.7), channel_id=1, source_target_pairs={{0,1},{1,0},{2,3},{3,2},{4,5},{5,4},{6,7},{7,6},{8,9},{9,8},{10,11... | collective-permute-start | bytes 12582920 | tf_op jit(solution)/shard_map/ppermute | solution.py:450
  2.2 29.1 %collective-permute-start.2 = (f32[960,512]{1,0:T(8,128)S(1)}, f32[960,512]{1,0:T(8,128)}, u32[]{:S(2)}, u32[]{:S(2)}) collective-permute-start(f32[960,512]{1,0:T(8,128)S(1)} %copy_kernel.1.sent), channel_id=1, source_target_pairs={{1,2},{2,1},{3,4},{4,3},{5,6},{6,5},{7,8},{8,7},{9,10},{10,9},{11,... | collective-permute-start | bytes 5898248 | tf_op jit(solution)/shard_map/ppermute | solution.py:449
  12.0 13.5 %all-to-all-start = ((f32[16,16,128]{2,1,0:T(8,128)}), f32[16,16,128]{2,1,0:T(8,128)S(1)}, u32[]{:S(2)}, u32[]{:S(2)}) async-start(f32[16,16,128]{2,1,0:T(8,128)} %get-tuple-element.23), calls=%async_computation | async-start | bytes 262144 | tf_op jit(solution)/shard_map/all_to_all | solution.py:471
  18.7 6.7 %copy-start = (f32[512,64]{0,1:T(8,128)S(1)}, f32[512,64]{0,1:T(8,128)}, u32[]{:S(2)}) copy-start(f32[512,64]{0,1:T(8,128)} %param.5) | copy-start | bytes 393220
  25.5 4.1 %collective-permute-start.1 = (f32[72,512]{1,0:T(8,128)S(1)}, f32[72,512]{1,0:T(8,128)S(1)}, u32[]{:S(2)}, u32[]{:S(2)}) collective-permute-start(f32[72,512]{1,0:T(8,128)S(1)} %get-tuple-element.25.own), channel_id=1, source_target_pairs={{0,1},{1,0},{2,3},{3,2},{4,5},{5,4},{6,7},{7,6},{8,9},{9,8},{10,11... | collective-permute-start | bytes 442376 | tf_op jit(solution)/shard_map/ppermute | solution.py:495
  25.6 9.1 %collective-permute-start.3 = (f32[136,512]{1,0:T(8,128)S(1)}, f32[136,512]{1,0:T(8,128)S(1)}, u32[]{:S(2)}, u32[]{:S(2)}) collective-permute-start(f32[136,512]{1,0:T(8,128)S(1)} %get-tuple-element.31), channel_id=1, source_target_pairs={{1,2},{2,1},{3,4},{4,3},{5,6},{6,5},{7,8},{8,7},{9,10},{10,9},{11,... | collective-permute-start | bytes 835592 | tf_op jit(solution)/shard_map/ppermute | solution.py:494
  29.6 1.9 %copy-start.1 = (f32[512,512]{1,0:T(8,128)S(1)}, f32[512,512]{1,0:T(8,128)}, u32[]{:S(2)}) copy-start(f32[512,512]{1,0:T(8,128)} %get-tuple-element.27.own_products) | copy-start | bytes 3145732

commit v5 on v4

--- a/solution.py
+++ b/solution.py
@@ -377,6 +377,8 @@
         parts = values.reshape(count, 2, piece_rows, columns)
         return jnp.concatenate([parts[:, 0], parts[:, 1]], axis=-1)
 
+    at_end = (block == 0) | (block == lax.axis_size("snp") - 1)
+    far_factor = jnp.where(at_end, 0.0, 1.0 / total)
     far_sum[...] = jnp.zeros_like(far_sum)
 
     def work(blocks, right_side):
@@ -401,7 +403,7 @@
 
     in_triangle(width, odd == 1, work)
     out[:, 1 - odd] = pieces_of(own_sum[...] * row_scale)
-    out[:, odd] = pieces_of((far_sum[...] * (far_scale * (1.0 / total))).T)
+    out[:, odd] = pieces_of((far_sum[...] * (far_scale * far_factor)).T)
 
 
 def last_kernel(parts, out):
@@ -438,7 +440,7 @@
     gram_flops = 6 * width * width * samples_here
     chip_pairs = [(i, i ^ 1) for i in range(snp_count)]
     cross = [(i, (i + 1) % snp_count) for i in range(1, snp_count, 2)]
-    cross_pairs = [pair for i, j in cross[:-1] for pair in ((i, j), (j, i))]
+    cross_pairs = [pair for i, j in cross for pair in ((i, j), (j, i))]
     effect_rows = effect.T
     square = (width, width)
     whole = (samples_here, width)

time: 55 us -> 53.2 us (0.967)
  starting transfers between devices: 16.1 us -> 12.7 us
  blocking collectives: 17.1 us -> 18.8 us
    ppermute x1, starting transfers between devices: 4.65 us -> 2.82 us  [body(): across = lax.ppermute(sent, 'snp', cross_pairs)]
    ppermute x1, starting transfers between devices: 3.95 us -> 2.13 us  [body(): far = lax.ppermute(later, 'snp', cross_pairs)]
    all_to_all x1, blocking collectives: 17.1 us -> 18.8 us  [body(): lax.all_to_all(sums.reshape(2 * samp_count, row_count // 2, 2 * columns),...]
  transfers between devices with their start and end apart: 5 -> 5, of which waited for: 2 -> 2; matrix products, arithmetic and copies ran while one was open for 0% -> 0% of each run, Pallas kernels for 31% -> 32%
where the time goes in v5:
time: 53.2 us; the launch traced here: 52.9 us
  Pallas kernels  20.1 us (38%)
  blocking collectives  18.8 us (35%)
  starting transfers between devices  12.7 us (24%)
  waiting for transfers between devices  1.09 us (2%)
    all_to_all x1, blocking collectives, body(): lax.all_to_all(sums.reshape(2 * samp_count, row_count // 2, 2 * columns),...  18.8 us
    all_to_all x1, starting transfers between devices, body(): packs = lax.all_to_all(pack, 'samp', 0, 0)  6.77 us
    pallas_call x1, Pallas kernels, body(): call(mate_kernel, [square, (8, width), pltpu.HBM(square, F32), (LAST_ROWS...  5.67 us
    pallas_call x1, Pallas kernels, body(): call(stat_kernel, [(samp_count, 4 * width // LANES, LANES), (8, width), s...  5.09 us
    pallas_call x1, Pallas kernels, body(): call(cross_kernel, [square, (8, width), (width, columns)], [VMEM, VMEM, H...  3.19 us
    ppermute x1, starting transfers between devices, body(): across = lax.ppermute(sent, 'snp', cross_pairs)  2.82 us
    pallas_call x1, Pallas kernels, body(): call(far_kernel, [(samp_count, 2, row_count // 2, 2 * columns)], [VMEM] *...  2.18 us
    ppermute x1, starting transfers between devices, body(): far = lax.ppermute(later, 'snp', cross_pairs)  2.13 us
  transfers between devices with their start and end apart: 5, of which 2 were waited for; matrix products, arithmetic and copies ran while one was open for 0% of the time, Pallas kernels for 32%

profile of v5, /device:TPU:97, one launch (start us, length us, event | category | flops | bytes accessed | tf_op | source)
XLA Modules:
  0.0 52.9 jit_solution(8936230761281886136)
XLA Ops:
  0.0 0.7 %collective-permute-start = (f32[2048,512]{1,0:T(8,128)}, f32[2048,512]{1,0:T(8,128)}, u32[]{:S(2)}, u32[]{:S(2)}) collective-permute-start(f32[2048,512]{1,0:T(8,128)} %geno.7), channel_id=1, source_target_pairs={{0,1},{1,0},{2,3},{3,2},{4,5},{5,4},{6,7},{7,6},{8,9},{9,8},{10,11... | collective-permute-start | bytes 12582920 | tf_op jit(solution)/shard_map/ppermute | solution.py:452
  0.7 1.5 %copy_kernel.1.sent = f32[960,512]{1,0:T(8,128)S(1)} custom-call(f32[2048,512]{1,0:T(8,128)} %geno.7), custom_call_target="tpu_custom_call" | custom-call | flops 1000 | bytes 1000 | tf_op jit(solution)/shard_map/copy_kernel/pallas_call | solution.py:450
  2.2 2.8 %collective-permute-start.2 = (f32[960,512]{1,0:T(8,128)S(1)}, f32[960,512]{1,0:T(8,128)}, u32[]{:S(2)}, u32[]{:S(2)}) collective-permute-start(f32[960,512]{1,0:T(8,128)S(1)} %copy_kernel.1.sent), channel_id=1, source_target_pairs={{1,2},{2,1},{3,4},{4,3},{5,6},{6,5},{7,8},{8,7},{9,10},{10,9},{11,... | collective-permute-start | bytes 5898248 | tf_op jit(solution)/shard_map/ppermute | solution.py:451
  5.0 5.1 %stat_kernel.1 = (f32[16,16,128]{2,1,0:T(8,128)}, f32[8,512]{1,0:T(8,128)S(1)}, f32[512,512]{1,0:T(8,128)S(1)}) custom-call(f32[2048,512]{1,0:T(8,128)} %geno.7, s32[1,32]{1,0:T(1,128)} %bitcast.6, s32[1,32]{1,0:T(1,128)} %bitcast.7, f32[960,512]{1,0:T(8,128)S(1)} %copy_kernel.1.sent), custom_call_target="tpu_custom_call" | custom-call | flops 1000 | bytes 1000 | tf_op jit(solution)/shard_map/stat_kernel/pallas_call | solution.py:453
  10.1 6.8 %all-to-all-start = ((f32[16,16,128]{2,1,0:T(8,128)}), f32[16,16,128]{2,1,0:T(8,128)S(1)}, u32[]{:S(2)}, u32[]{:S(2)}) async-start(f32[16,16,128]{2,1,0:T(8,128)} %get-tuple-element.23), calls=%async_computation | async-start | bytes 262144 | tf_op jit(solution)/shard_map/all_to_all | solution.py:473
  16.9 0.0 collective-permute-done.mate
  16.9 0.0 copy-start
  16.9 5.7 %mate_kernel.1 = (f32[512,512]{1,0:T(8,128)S(1)}, f32[8,512]{1,0:T(8,128)S(1)}, f32[512,512]{1,0:T(8,128)}, f32[64,512]{1,0:T(8,128)S(1)}) custom-call(f32[2048,512]{1,0:T(8,128)} %geno.7, f32[2048,512]{1,0:T(8,128)} %collective-permute-done.mate, f32[8,512]{1,0:T(8,128)S(1)} %get-tuple-element.19.means, ...), custom_call_target="tpu_custom_call", output_to_operand_aliasing={{0}: (3, {})} | custom-call | flops 6442450944 | bytes 1000 | tf_op jit(solution)/shard_map/mate_kernel/pallas_call | solution.py:474
  22.6 1.0 %all-to-all-done.packs = f32[16,16,128]{2,1,0:T(8,128)S(1)} async-done(((f32[16,16,128]{2,1,0:T(8,128)}), f32[16,16,128]{2,1,0:T(8,128)S(1)}, u32[]{:S(2)}, u32[]{:S(2)}) %all-to-all-start) | async-done | bytes 131104 | tf_op jit(solution)/shard_map/all_to_all | solution.py:473
  23.6 0.0 copy-done
  23.6 0.1 combine_kernel.1
  23.7 0.3 collective-permute-start.1
  23.9 2.1 %collective-permute-start.3 = (f32[136,512]{1,0:T(8,128)S(1)}, f32[136,512]{1,0:T(8,128)S(1)}, u32[]{:S(2)}, u32[]{:S(2)}) collective-permute-start(f32[136,512]{1,0:T(8,128)S(1)} %get-tuple-element.31), channel_id=1, source_target_pairs={{1,2},{2,1},{3,4},{4,3},{5,6},{6,5},{7,8},{8,7},{9,10},{10,9},{11,... | collective-permute-start | bytes 835592 | tf_op jit(solution)/shard_map/ppermute | solution.py:496
  26.1 0.0 collective-permute-done.1.mate
  26.1 0.0 copy-start.1
  26.1 1.7 %near_kernel.1 = (f32[512,64]{1,0:T(8,128)S(1)}, f32[1024,512]{1,0:T(8,128)S(1)}) custom-call(f32[2048,512]{1,0:T(8,128)} %geno.7, f32[8,512]{1,0:T(8,128)S(1)} %get-tuple-element.19.means, f32[512,512]{1,0:T(8,128)S(1)} %get-tuple-element.21.mate_products, f32[8,512]{1,0:T(8,128)S(1)} %get-tuple-element.22.mate_means, f32[72,512]{1,0:T(8,128)S(1)} %get-tuple-element.25.own, ...), custom_call_target="tpu_custom_call" | custom-call | flops 1000 | bytes 1000 | tf_op jit(solution)/shard_map/near_kernel/pallas_call | solution.py:498
  27.7 0.0 collective-permute-done.2.across
  27.7 0.2 copy-done.1
  27.9 3.2 %cross_kernel.1 = (f32[512,512]{1,0:T(8,128)S(1)}, f32[8,512]{1,0:T(8,128)S(1)}, f32[512,64]{1,0:T(8,128)S(1)}) custom-call(f32[1024,512]{1,0:T(8,128)S(1)} %get-tuple-element.26.kept, f32[8,512]{1,0:T(8,128)S(1)} %get-tuple-element.19.means, f32[960,512]{1,0:T(8,128)} %collective-permute-done.2.across, f32[512,512]{1,0:T(8,128)S(1)} %copy-done.1, ...), custom_call_target="tpu_custom_call" | custom-call | flops 3221225472 | bytes 1000 | tf_op jit(solution)/shard_map/cross_kernel/pallas_call | solution.py:506
  31.1 0.1 collective-permute-done.3.later
  31.2 2.2 %far_kernel.1 = f32[16,2,16,128]{3,2,1,0:T(8,128)S(1)} custom-call(f32[1024,512]{1,0:T(8,128)S(1)} %get-tuple-element.26.kept, f32[512,512]{1,0:T(8,128)S(1)} %get-tuple-element.29.products, f32[8,512]{1,0:T(8,128)S(1)} %get-tuple-element.19.means, f32[8,512]{1,0:T(8,128)S(1)} %get-tuple-element.30.cross_means, f32[136,512]{1,0:T(8,128)S(1)} %collective-permute-done.3.later, ...), custom_call_target="tpu_custom_call" | custom-call | flops 1000 | bytes 1000 | tf_op jit(solution)/shard_map/far_kernel/pallas_call | solution.py:515
  33.4 18.8 %all_to_all.10.parts = f32[32,16,128]{2,1,0:T(8,128)S(1)} all-to-all(f32[32,16,128]{2,1,0:T(8,128)S(1)} %bitcast.4), channel_id=1, replica_groups={{1,2,17,18,33,34,49,50,65,66,81,82,97,98,113,114,129,130,145,146,161,16..., dimensions={0} | all-to-all | bytes 524288 | tf_op jit(solution)/shard_map/all_to_all | solution.py:524
  52.2 0.7 %last_kernel.1 = f32[32,64]{1,0:T(8,128)} custom-call(f32[32,16,128]{2,1,0:T(8,128)S(1)} %all_to_all.10.parts), custom_call_target="tpu_custom_call" | custom-call | flops 1000 | bytes 1000 | tf_op jit(solution)/shard_map/last_kernel/pallas_call | solution.py:531
Async XLA Ops:
  0.0 16.9 %collective-permute-start = (f32[2048,512]{1,0:T(8,128)}, f32[2048,512]{1,0:T(8,128)}, u32[]{:S(2)}, u32[]{:S(2)}) collective-permute-start(f32[2048,512]{1,0:T(8,128)} %geno.7), channel_id=1, source_target_pairs={{0,1},{1,0},{2,3},{3,2},{4,5},{5,4},{6,7},{7,6},{8,9},{9,8},{10,11... | collective-permute-start | bytes 12582920 | tf_op jit(solution)/shard_map/ppermute | solution.py:452
  2.2 25.6 %collective-permute-start.2 = (f32[960,512]{1,0:T(8,128)S(1)}, f32[960,512]{1,0:T(8,128)}, u32[]{:S(2)}, u32[]{:S(2)}) collective-permute-start(f32[960,512]{1,0:T(8,128)S(1)} %copy_kernel.1.sent), channel_id=1, source_target_pairs={{1,2},{2,1},{3,4},{4,3},{5,6},{6,5},{7,8},{8,7},{9,10},{10,9},{11,... | collective-permute-start | bytes 5898248 | tf_op jit(solution)/shard_map/ppermute | solution.py:451
  10.1 13.5 %all-to-all-start = ((f32[16,16,128]{2,1,0:T(8,128)}), f32[16,16,128]{2,1,0:T(8,128)S(1)}, u32[]{:S(2)}, u32[]{:S(2)}) async-start(f32[16,16,128]{2,1,0:T(8,128)} %get-tuple-element.23), calls=%async_computation | async-start | bytes 262144 | tf_op jit(solution)/shard_map/all_to_all | solution.py:473
  16.9 6.7 %copy-start = (f32[512,64]{0,1:T(8,128)S(1)}, f32[512,64]{0,1:T(8,128)}, u32[]{:S(2)}) copy-start(f32[512,64]{0,1:T(8,128)} %param.5) | copy-start | bytes 393220
  23.7 2.4 %collective-permute-start.1 = (f32[72,512]{1,0:T(8,128)S(1)}, f32[72,512]{1,0:T(8,128)S(1)}, u32[]{:S(2)}, u32[]{:S(2)}) collective-permute-start(f32[72,512]{1,0:T(8,128)S(1)} %get-tuple-element.25.own), channel_id=1, source_target_pairs={{0,1},{1,0},{2,3},{3,2},{4,5},{5,4},{6,7},{7,6},{8,9},{9,8},{10,11... | collective-permute-start | bytes 442376 | tf_op jit(solution)/shard_map/ppermute | solution.py:497
  23.9 7.3 %collective-permute-start.3 = (f32[136,512]{1,0:T(8,128)S(1)}, f32[136,512]{1,0:T(8,128)S(1)}, u32[]{:S(2)}, u32[]{:S(2)}) collective-permute-start(f32[136,512]{1,0:T(8,128)S(1)} %get-tuple-element.31), channel_id=1, source_target_pairs={{1,2},{2,1},{3,4},{4,3},{5,6},{6,5},{7,8},{8,7},{9,10},{10,9},{11,... | collective-permute-start | bytes 835592 | tf_op jit(solution)/shard_map/ppermute | solution.py:496
  26.1 1.9 %copy-start.1 = (f32[512,512]{1,0:T(8,128)S(1)}, f32[512,512]{1,0:T(8,128)}, u32[]{:S(2)}) copy-start(f32[512,512]{1,0:T(8,128)} %get-tuple-element.27.own_products) | copy-start | bytes 3145732

commit v6 on v5

--- a/solution.py
+++ b/solution.py
@@ -260,7 +260,7 @@
 ):
     width = mate_products.shape[0]
     block, odd, _, kept_at = position(samples_here)
-    kept_copies = copies_in(geno, kept_at, kept, kept_sems, 2)
+    kept_copies = copies_in(geno, kept_at, kept, kept_sems, 1)
     start(kept_copies)
     info = own[columns : columns + 4]
     shift = means[0:1] - info[0:1]
@@ -282,7 +282,8 @@
 
 
 def cross_kernel(
-    kept,
+    geno,
+    kept_first,
     means,
     across,
     own_products,
@@ -291,18 +292,21 @@
     products,
     cross_means,
     near_sum,
+    kept_last,
     others,
     sems,
+    kept_sems,
     *,
     columns,
     samples_here,
 ):
     rows, width = others.shape
-    block, odd = position(rows)[:2]
+    block, odd, _, kept_at = position(geno.shape[0])
     pieces = sems.shape[0]
     piece = rows // pieces
     copies = copies_in(across, 0, others, sems, pieces)
-    start(copies)
+    kept_copies = copies_in(geno, kept_at + piece, kept_last, kept_sems, 1)
+    start(copies, kept_copies)
     mean = means[0:1]
     info = own[columns : columns + 4]
     shift = mean - info[0:1]
@@ -314,13 +318,15 @@
     centre = None
     for i, copy in enumerate(copies):
         copy.wait()
+        if i == 1:
+            finish(*kept_copies)
         at = slice(i * piece, (i + 1) * piece)
         part = column_sum(others[at])
         other_sum = part if i == 0 else other_sum + part
         centre = part / piece if i == 0 else centre
 
         def work(blocks, right_side):
-            left = kept[at] - mean
+            left = (kept_last[:piece] if i else kept_first[...]) - mean
             total = column_sum(left)
             if i == 0:
                 cross_means[0:1] = total
@@ -354,11 +360,12 @@
     *,
     columns,
     total,
+    samples_here,
 ):
-    half, width = kept.shape
+    half, width = samples_here // 2, own.shape[1]
     rows = later.shape[0] - own.shape[0]
     first_rows = half - rows
-    block, odd = position(half)[:2]
+    block, odd = position(samples_here)[:2]
     mean = own[columns : columns + 1]
     info = later[rows + columns : rows + columns + 4]
     far_mean, far_scale = info[0:1], info[1:2]
@@ -371,7 +378,7 @@
     centre_shift = cross_means[2:3] - far_mean
     other_shift = cross_means[1:2] - far_mean
     far_block = block + 2 * odd - 1
-    count, _, piece_rows, lanes = out.shape
+    _, count, piece_rows, lanes = out.shape
 
     def pieces_of(values):
         parts = values.reshape(count, 2, piece_rows, columns)
@@ -382,7 +389,7 @@
     far_sum[...] = jnp.zeros_like(far_sum)
 
     def work(blocks, right_side):
-        left, right = split(kept[first_rows:] - mean), split(later[:rows] - far_mean)
+        left, right = split(kept[kept.shape[0] - rows :] - mean), split(later[:rows] - far_mean)
         for at, cols in blocks:
             centred = products[at, cols] + block_dots(left, right, at, cols)
             centred = centred + left_sum[at] * centre_shift[:, cols]
@@ -402,8 +409,8 @@
             far_sum[:, cols] += three_dots(split(own[:columns, at]), split(far_band), 1, 0)
 
     in_triangle(width, odd == 1, work)
-    out[:, 1 - odd] = pieces_of(own_sum[...] * row_scale)
-    out[:, odd] = pieces_of((far_sum[...] * (far_scale * far_factor)).T)
+    out[1 - odd] = pieces_of(own_sum[...] * row_scale)
+    out[odd] = pieces_of((far_sum[...] * (far_scale * far_factor)).T)
 
 
 def last_kernel(parts, out):
@@ -495,32 +502,38 @@
     )(packs, effect_rows, sent_last)
     far = lax.ppermute(later, "snp", cross_pairs)
     mate_info = lax.ppermute(own, "snp", chip_pairs)
+    piece_rows = (half - LAST_ROWS) // FAR_READS
     near, kept = call(
         near_kernel,
-        [(width, columns), (half, width)],
+        [(width, columns), (piece_rows, width)],
         [HBM] + [VMEM] * 5,
-        [pltpu.SemaphoreType.DMA((2,))],
+        [pltpu.SemaphoreType.DMA((1,))],
         columns=columns,
         samples_here=samples_here,
     )(in_hbm, means, mate_products, mate_means, own, mate_info)
-    cross_products, cross_means, near = call(
+    cross_products, cross_means, near, kept = call(
         cross_kernel,
-        [square, (8, width), (width, columns)],
-        [VMEM, VMEM, HBM] + [VMEM] * 3,
-        [pltpu.VMEM((half - LAST_ROWS, width), F32), pltpu.SemaphoreType.DMA((FAR_READS,))],
+        [square, (8, width), (width, columns), (half - piece_rows, width)],
+        [HBM, VMEM, VMEM, HBM] + [VMEM] * 3,
+        [
+            pltpu.VMEM((half - LAST_ROWS, width), F32),
+            pltpu.SemaphoreType.DMA((FAR_READS,)),
+            pltpu.SemaphoreType.DMA((1,)),
+        ],
         columns=columns,
         samples_here=samples_here,
         flops=gram_flops,
-    )(kept, means, pltpu.with_memory_space_constraint(across, pltpu.HBM), own_products, own, near)
+    )(in_hbm, kept, means, pltpu.with_memory_space_constraint(across, pltpu.HBM), own_products, own, near)
     sums = call(
         far_kernel,
-        [(samp_count, 2, row_count // 2, 2 * columns)],
+        [(2, samp_count, row_count // 2, 2 * columns)],
         [VMEM] * 7,
         [pltpu.VMEM((width, columns), F32), pltpu.VMEM((columns, width), F32)],
         columns=columns,
         total=total,
+        samples_here=samples_here,
     )(kept, cross_products, means, cross_means, far, own, near)[0]
-    groups = [[s * snp_count + i for s in range(samp_count) for i in pair] for pair in cross]
+    groups = [[s * snp_count + i for i in pair for s in range(samp_count)] for pair in cross]
     parts = lax.all_to_all(
         sums.reshape(2 * samp_count, row_count // 2, 2 * columns),
         ("samp", "snp"),

time: 53.2 us -> 52.9 us (level)
  transfers between devices with their start and end apart: 5 -> 5, of which waited for: 2 -> 3; matrix products, arithmetic and copies ran while one was open for 0% -> 0% of each run, Pallas kernels for 32% -> 32%
where the time goes in v6:
time: 52.9 us; the launch traced here: 52.6 us
  Pallas kernels  19.7 us (37%)
  blocking collectives  18.5 us (35%)
  starting transfers between devices  12.7 us (24%)
  waiting for transfers between devices  1.62 us (3%)
    all_to_all x1, blocking collectives, body(): lax.all_to_all(sums.reshape(2 * samp_count, row_count // 2, 2 * columns),...  18.5 us
    all_to_all x1, starting transfers between devices, body(): packs = lax.all_to_all(pack, 'samp', 0, 0)  6.77 us
    pallas_call x1, Pallas kernels, body(): call(mate_kernel, [square, (8, width), pltpu.HBM(square, F32), (LAST_ROWS...  5.67 us
    pallas_call x1, Pallas kernels, body(): call(stat_kernel, [(samp_count, 4 * width // LANES, LANES), (8, width), s...  5.09 us
    pallas_call x1, Pallas kernels, body(): call(cross_kernel, [square, (8, width), (width, columns), (half - piece_r...  3.19 us
    ppermute x1, starting transfers between devices, body(): across = lax.ppermute(sent, 'snp', cross_pairs)  2.82 us
    pallas_call x1, Pallas kernels, body(): call(far_kernel, [(2, samp_count, row_count // 2, 2 * columns)], [VMEM] *...  2.18 us
    ppermute x1, starting transfers between devices, body(): far = lax.ppermute(later, 'snp', cross_pairs)  2.13 us
  transfers between devices with their start and end apart: 5, of which 3 were waited for; matrix products, arithmetic and copies ran while one was open for 0% of the time, Pallas kernels for 32%

profile of v6, /device:TPU:97, one launch (start us, length us, event | category | flops | bytes accessed | tf_op | source)
XLA Modules:
  0.0 52.6 jit_solution(17956521675840414535)
XLA Ops:
  0.0 0.7 %collective-permute-start = (f32[2048,512]{1,0:T(8,128)}, f32[2048,512]{1,0:T(8,128)}, u32[]{:S(2)}, u32[]{:S(2)}) collective-permute-start(f32[2048,512]{1,0:T(8,128)} %geno.9), channel_id=1, source_target_pairs={{0,1},{1,0},{2,3},{3,2},{4,5},{5,4},{6,7},{7,6},{8,9},{9,8},{10,11... | collective-permute-start | bytes 12582920 | tf_op jit(solution)/shard_map/ppermute | solution.py:459
  0.7 1.5 %copy_kernel.1.sent = f32[960,512]{1,0:T(8,128)S(1)} custom-call(f32[2048,512]{1,0:T(8,128)} %geno.9), custom_call_target="tpu_custom_call" | custom-call | flops 1000 | bytes 1000 | tf_op jit(solution)/shard_map/copy_kernel/pallas_call | solution.py:457
  2.2 2.8 %collective-permute-start.2 = (f32[960,512]{1,0:T(8,128)S(1)}, f32[960,512]{1,0:T(8,128)}, u32[]{:S(2)}, u32[]{:S(2)}) collective-permute-start(f32[960,512]{1,0:T(8,128)S(1)} %copy_kernel.1.sent), channel_id=1, source_target_pairs={{1,2},{2,1},{3,4},{4,3},{5,6},{6,5},{7,8},{8,7},{9,10},{10,9},{11,... | collective-permute-start | bytes 5898248 | tf_op jit(solution)/shard_map/ppermute | solution.py:458
  5.0 5.1 %stat_kernel.1 = (f32[16,16,128]{2,1,0:T(8,128)}, f32[8,512]{1,0:T(8,128)S(1)}, f32[512,512]{1,0:T(8,128)S(1)}) custom-call(f32[2048,512]{1,0:T(8,128)} %geno.9, s32[1,32]{1,0:T(1,128)} %bitcast.6, s32[1,32]{1,0:T(1,128)} %bitcast.7, f32[960,512]{1,0:T(8,128)S(1)} %copy_kernel.1.sent), custom_call_target="tpu_custom_call" | custom-call | flops 1000 | bytes 1000 | tf_op jit(solution)/shard_map/stat_kernel/pallas_call | solution.py:460
  10.1 6.8 %all-to-all-start = ((f32[16,16,128]{2,1,0:T(8,128)}), f32[16,16,128]{2,1,0:T(8,128)S(1)}, u32[]{:S(2)}, u32[]{:S(2)}) async-start(f32[16,16,128]{2,1,0:T(8,128)} %get-tuple-element.24), calls=%async_computation | async-start | bytes 262144 | tf_op jit(solution)/shard_map/all_to_all | solution.py:480
  16.9 0.0 collective-permute-done.mate
  16.9 0.0 copy-start
  16.9 5.7 %mate_kernel.1 = (f32[512,512]{1,0:T(8,128)S(1)}, f32[8,512]{1,0:T(8,128)S(1)}, f32[512,512]{1,0:T(8,128)}, f32[64,512]{1,0:T(8,128)S(1)}) custom-call(f32[2048,512]{1,0:T(8,128)} %geno.9, f32[2048,512]{1,0:T(8,128)} %collective-permute-done.mate, f32[8,512]{1,0:T(8,128)S(1)} %get-tuple-element.20.means, ...), custom_call_target="tpu_custom_call", output_to_operand_aliasing={{0}: (3, {})} | custom-call | flops 6442450944 | bytes 1000 | tf_op jit(solution)/shard_map/mate_kernel/pallas_call | solution.py:481
  22.6 1.0 %all-to-all-done.packs = f32[16,16,128]{2,1,0:T(8,128)S(1)} async-done(((f32[16,16,128]{2,1,0:T(8,128)}), f32[16,16,128]{2,1,0:T(8,128)S(1)}, u32[]{:S(2)}, u32[]{:S(2)}) %all-to-all-start) | async-done | bytes 131104 | tf_op jit(solution)/shard_map/all_to_all | solution.py:480
  23.6 0.0 copy-done
  23.6 0.1 combine_kernel.1
  23.7 0.3 collective-permute-start.1
  23.9 2.1 %collective-permute-start.3 = (f32[136,512]{1,0:T(8,128)S(1)}, f32[136,512]{1,0:T(8,128)S(1)}, u32[]{:S(2)}, u32[]{:S(2)}) collective-permute-start(f32[136,512]{1,0:T(8,128)S(1)} %get-tuple-element.33), channel_id=1, source_target_pairs={{1,2},{2,1},{3,4},{4,3},{5,6},{6,5},{7,8},{8,7},{9,10},{10,9},{11,... | collective-permute-start | bytes 835592 | tf_op jit(solution)/shard_map/ppermute | solution.py:503
  26.1 0.0 collective-permute-done.1.mate
  26.1 0.0 copy-start.1
  26.1 1.3 %near_kernel.1 = (f32[512,64]{1,0:T(8,128)S(1)}, f32[480,512]{1,0:T(8,128)S(1)}) custom-call(f32[2048,512]{1,0:T(8,128)} %geno.9, f32[8,512]{1,0:T(8,128)S(1)} %get-tuple-element.20.means, f32[512,512]{1,0:T(8,128)S(1)} %get-tuple-element.22.mate_products, f32[8,512]{1,0:T(8,128)S(1)} %get-tuple-element.23.mate_means, f32[72,512]{1,0:T(8,128)S(1)} %get-tuple-element.26.own, ...), custom_call_target="tpu_custom_call" | custom-call | flops 1000 | bytes 1000 | tf_op jit(solution)/shard_map/near_kernel/pallas_call | solution.py:506
  27.4 0.3 collective-permute-done.2.across
  27.6 0.0 copy-done.1
  27.7 3.2 %cross_kernel.1 = (f32[512,512]{1,0:T(8,128)S(1)}, f32[8,512]{1,0:T(8,128)S(1)}, f32[512,64]{1,0:T(8,128)S(1)}, f32[544,512]{1,0:T(8,128)S(1)}) custom-call(f32[2048,512]{1,0:T(8,128)} %geno.9, f32[480,512]{1,0:T(8,128)S(1)} %get-tuple-element.27.kept_first, f32[8,512]{1,0:T(8,128)S(1)} %get-tuple-element.20.means, ...), custom_call_target="tpu_custom_call" | custom-call | flops 3221225472 | bytes 1000 | tf_op jit(solution)/shard_map/cross_kernel/pallas_call | solution.py:514
  30.8 0.4 collective-permute-done.3.later
  31.2 2.2 %far_kernel.1 = f32[2,16,16,128]{3,2,1,0:T(8,128)S(1)} custom-call(f32[544,512]{1,0:T(8,128)S(1)} %get-tuple-element.30.kept, f32[512,512]{1,0:T(8,128)S(1)} %get-tuple-element.31.products, f32[8,512]{1,0:T(8,128)S(1)} %get-tuple-element.20.means, f32[8,512]{1,0:T(8,128)S(1)} %get-tuple-element.32.cross_means, f32[136,512]{1,0:T(8,128)S(1)} %collective-permute-done.3.later, ...), custom_call_target="tpu_custom_call" | custom-call | flops 1000 | bytes 1000 | tf_op jit(solution)/shard_map/far_kernel/pallas_call | solution.py:527
  33.4 18.5 %all_to_all.10.parts = f32[32,16,128]{2,1,0:T(8,128)S(1)} all-to-all(f32[32,16,128]{2,1,0:T(8,128)S(1)} %bitcast.4), channel_id=1, replica_groups={{1,17,33,49,65,81,97,113,129,145,161,177,193,209,225,241,2,18,34,50,66,..., dimensions={0} | all-to-all | bytes 524288 | tf_op jit(solution)/shard_map/all_to_all | solution.py:537
  51.9 0.7 %last_kernel.1 = f32[32,64]{1,0:T(8,128)} custom-call(f32[32,16,128]{2,1,0:T(8,128)S(1)} %all_to_all.10.parts), custom_call_target="tpu_custom_call" | custom-call | flops 1000 | bytes 1000 | tf_op jit(solution)/shard_map/last_kernel/pallas_call | solution.py:544
Async XLA Ops:
  0.0 16.9 %collective-permute-start = (f32[2048,512]{1,0:T(8,128)}, f32[2048,512]{1,0:T(8,128)}, u32[]{:S(2)}, u32[]{:S(2)}) collective-permute-start(f32[2048,512]{1,0:T(8,128)} %geno.9), channel_id=1, source_target_pairs={{0,1},{1,0},{2,3},{3,2},{4,5},{5,4},{6,7},{7,6},{8,9},{9,8},{10,11... | collective-permute-start | bytes 12582920 | tf_op jit(solution)/shard_map/ppermute | solution.py:459
  2.2 25.5 %collective-permute-start.2 = (f32[960,512]{1,0:T(8,128)S(1)}, f32[960,512]{1,0:T(8,128)}, u32[]{:S(2)}, u32[]{:S(2)}) collective-permute-start(f32[960,512]{1,0:T(8,128)S(1)} %copy_kernel.1.sent), channel_id=1, source_target_pairs={{1,2},{2,1},{3,4},{4,3},{5,6},{6,5},{7,8},{8,7},{9,10},{10,9},{11,... | collective-permute-start | bytes 5898248 | tf_op jit(solution)/shard_map/ppermute | solution.py:458
  10.1 13.5 %all-to-all-start = ((f32[16,16,128]{2,1,0:T(8,128)}), f32[16,16,128]{2,1,0:T(8,128)S(1)}, u32[]{:S(2)}, u32[]{:S(2)}) async-start(f32[16,16,128]{2,1,0:T(8,128)} %get-tuple-element.24), calls=%async_computation | async-start | bytes 262144 | tf_op jit(solution)/shard_map/all_to_all | solution.py:480
  16.9 6.7 %copy-start = (f32[512,64]{0,1:T(8,128)S(1)}, f32[512,64]{0,1:T(8,128)}, u32[]{:S(2)}) copy-start(f32[512,64]{0,1:T(8,128)} %param.5) | copy-start | bytes 393220
  23.7 2.4 %collective-permute-start.1 = (f32[72,512]{1,0:T(8,128)S(1)}, f32[72,512]{1,0:T(8,128)S(1)}, u32[]{:S(2)}, u32[]{:S(2)}) collective-permute-start(f32[72,512]{1,0:T(8,128)S(1)} %get-tuple-element.26.own), channel_id=1, source_target_pairs={{0,1},{1,0},{2,3},{3,2},{4,5},{5,4},{6,7},{7,6},{8,9},{9,8},{10,11... | collective-permute-start | bytes 442376 | tf_op jit(solution)/shard_map/ppermute | solution.py:504
  23.9 7.3 %collective-permute-start.3 = (f32[136,512]{1,0:T(8,128)S(1)}, f32[136,512]{1,0:T(8,128)S(1)}, u32[]{:S(2)}, u32[]{:S(2)}) collective-permute-start(f32[136,512]{1,0:T(8,128)S(1)} %get-tuple-element.33), channel_id=1, source_target_pairs={{1,2},{2,1},{3,4},{4,3},{5,6},{6,5},{7,8},{8,7},{9,10},{10,9},{11,... | collective-permute-start | bytes 835592 | tf_op jit(solution)/shard_map/ppermute | solution.py:503
  26.1 1.6 %copy-start.1 = (f32[512,512]{1,0:T(8,128)S(1)}, f32[512,512]{1,0:T(8,128)}, u32[]{:S(2)}) copy-start(f32[512,512]{1,0:T(8,128)} %get-tuple-element.28.own_products) | copy-start | bytes 3145732
